TPU v7x, 32 devices: a whole 2x2x4 slice. The times are simulated.
32 devices in a mesh: rows: 8 (over z, core), tm: 4 (over y, x).
Axes of the slice: x: 2, y: 2, z: 4, core: 2. Of those that a mesh axis runs over, the one named last changes fastest.
Arguments:
- frames: bfloat16 [16, 1536, 512], P('rows', 'tm'), may hold values from -6 to 6
- cotangent: bfloat16 [16, 1536, 512], P('rows', 'tm'), may hold values from -6 to 6
- lengths: int32 [16], P('rows'), may hold values from 192 to 1536, as said below
- early_gain: bfloat16 [512], replicated, may hold values from 0.5 to 1.5
- early_shift: bfloat16 [512], replicated, may hold values from -3 to 3
- early_up: bfloat16 [512, 2048], replicated, may hold values from -0.25 to 0.25
- early_down: bfloat16 [2048, 512], replicated, may hold values from -0.125 to 0.125
- attend_gain: bfloat16 [512], replicated, may hold values from 0.5 to 1.5
- attend_shift: bfloat16 [512], replicated, may hold values from -3 to 3
- attend_input: bfloat16 [512, 1536], replicated, may hold values from -0.25 to 0.25
- attend_output: bfloat16 [512, 512], replicated, may hold values from -1 to 1
- distance_bias: bfloat16 [32, 8], replicated, may hold values from -4 to 4
- convolve_gain: bfloat16 [512], replicated, may hold values from 0.5 to 1.5
- convolve_shift: bfloat16 [512], replicated, may hold values from -3 to 3
- convolve_input: bfloat16 [512, 2048], replicated, may hold values from -0.25 to 0.25
- depthwise: bfloat16 [1024, 15], replicated, may hold values from -1.5 to 1.5
- inner_gain: bfloat16 [1024], replicated, may hold values from 0.5 to 1.5
- inner_shift: bfloat16 [1024], replicated, may hold values from -3 to 3
- convolve_output: bfloat16 [1024, 512], replicated, may hold values from -0.1875 to 0.1875
- late_gain: bfloat16 [512], replicated, may hold values from 0.5 to 1.5
- late_shift: bfloat16 [512], replicated, may hold values from -3 to 3
- late_up: bfloat16 [512, 2048], replicated, may hold values from -0.25 to 0.25
- late_down: bfloat16 [2048, 512], replicated, may hold values from -0.125 to 0.125
- final_gain: bfloat16 [512], replicated, may hold values from 0.5 to 1.5
- final_shift: bfloat16 [512], replicated, may hold values from -3 to 3
Outputs:
- layer_out: bfloat16 [16, 1536, 512], P('rows', 'tm')
- frames_gradient: bfloat16 [16, 1536, 512], P('rows', 'tm')
- early_gain_gradient: float32 [512], P('rows')
- early_shift_gradient: float32 [512], P('rows')
- early_up_gradient: float32 [512, 2048], P('rows')
- early_down_gradient: float32 [2048, 512], P('rows')
- attend_gain_gradient: float32 [512], P('rows')
- attend_shift_gradient: float32 [512], P('rows')
- attend_input_gradient: float32 [512, 1536], P('rows')
- attend_output_gradient: float32 [512, 512], P('rows')
- distance_bias_gradient: float32 [32, 8], P('rows')
- convolve_gain_gradient: float32 [512], P('rows')
- convolve_shift_gradient: float32 [512], P('rows')
- convolve_input_gradient: float32 [512, 2048], P('rows')
- depthwise_gradient: float32 [1024, 15], P('rows')
- inner_gain_gradient: float32 [1024], P('rows')
- inner_shift_gradient: float32 [1024], P('rows')
- convolve_output_gradient: float32 [1024, 512], P('rows')
- late_gain_gradient: float32 [512], P('rows')
- late_shift_gradient: float32 [512], P('rows')
- late_up_gradient: float32 [512, 2048], P('rows')
- late_down_gradient: float32 [2048, 512], P('rows')
- final_gain_gradient: float32 [512], P('rows')
- final_shift_gradient: float32 [512], P('rows')
Inputs may be any that keep to these rules, and one draw needn't show every extreme that they name: `lengths`: in every draw one recording has all 1536 frames valid and one has 192; shorter recordings are more common than longer ones.
All inputs are finite; a program needn't handle non-finite values.
Results may differ from a plain program's by a relative error of at most 0.02.
Values may be sent and summed in bfloat16 or wider, within the bound.
No kernel may reach another device: no remote copies, remote signals or barrier semaphores. Data moves between devices by JAX's collectives and lax.ppermute only.
A program may use at most 192 MiB of HBM per device.

v0:
```python
import jax
import jax.numpy as jnp
from jax import lax
from jax.sharding import PartitionSpec as P

EPSILON = 1e-05
NEGATIVE = -1e30
HIGHEST = lax.Precision.HIGHEST
BFLOAT = jnp.bfloat16
FLOAT = jnp.float32


def passed_along(block, axis, distance):
    devices = range(lax.axis_size(axis))
    route = [(i - distance, i) for i in devices if i - distance in devices]
    return lax.ppermute(block, axis, route)


def from_behind(value, axis, steps):
    count = lax.axis_size(axis)
    pairs = [(source, (source + steps) % count) for source in range(count)]
    return lax.ppermute(value, axis, pairs)


def boundaries(seq_total):
    edges_list = list(range(1, 16))
    for exponent in range(16):
        edges_list.append(int(16.0 * (seq_total / 16.0) ** (exponent / 16.0)))
    return edges_list


def layer_norm(inputs, norm_gain, norm_shift):
    center = inputs - jnp.mean(inputs, axis=-1, keepdims=True)
    variance = jnp.mean(center * center, axis=-1, keepdims=True)
    return center * lax.rsqrt(variance + EPSILON) * norm_gain + norm_shift


def norm_backward(inputs, norm_gain, norm_shift, grad_out):
    result, pullback = jax.vjp(layer_norm, inputs, norm_gain, norm_shift)
    return pullback(grad_out)


def dense(left_side, right_side):
    return jnp.dot(left_side, right_side, preferred_element_type=FLOAT)


def weight_grad(left_side, right_side):
    return lax.dot_general(
        left_side, right_side, (((0,), (0,)), ((), ())), preferred_element_type=FLOAT
    )


def input_grad(grad_values, weight):
    return lax.dot_general(
        grad_values, weight, (((1,), (1,)), ((), ())), preferred_element_type=FLOAT
    )


def ffn_forward(inputs, norm_gain, norm_shift, weight_up, weight_down):
    normed = layer_norm(inputs, norm_gain, norm_shift).astype(BFLOAT)
    hidden = dense(normed, weight_up)
    active = jax.nn.silu(hidden).astype(BFLOAT)
    return (dense(active, weight_down), (normed, hidden, active))


def ffn_backward(inputs, norm_gain, norm_shift, weight_up, weight_down, stored, grad_branch):
    normed, hidden, active = stored
    grad_rounded = grad_branch.astype(BFLOAT)
    grad_down = weight_grad(active, grad_rounded)
    grad_active = input_grad(grad_rounded, weight_down)
    grad_hidden = jax.vjp(jax.nn.silu, hidden)[1](grad_active)[0].astype(BFLOAT)
    grad_up = weight_grad(normed, grad_hidden)
    grad_normed = input_grad(grad_hidden, weight_up)
    grad_inputs, grad_gain, grad_shift = norm_backward(inputs, norm_gain, norm_shift, grad_normed)
    return (grad_inputs, (grad_gain, grad_shift, grad_up, grad_down))


def distance_onehot(bucket_count, query_first, key_last, query_count, key_count, seq_total):
    diag_span = query_count + key_count - 1
    distance = jnp.maximum(query_first - key_last + jnp.arange(diag_span, dtype=jnp.int32), 0)
    limits = jnp.array(boundaries(seq_total), jnp.int32)
    bucket = jnp.sum((distance[:, None] >= limits[None, :]).astype(jnp.int32), axis=1)
    return (bucket[:, None] == jnp.arange(bucket_count, dtype=jnp.int32)[None, :]).astype(FLOAT)


def expand_diagonals(per_distance, query_count, key_count):
    diag_span = query_count + key_count - 1
    tiled_rows = jnp.tile(per_distance[:, ::-1], (1, query_count))
    window = tiled_rows[:, query_count - 1 : query_count - 1 + query_count * (diag_span - 1)]
    return window.reshape(-1, query_count, diag_span - 1)[:, :, :key_count]


def sum_diagonals(grid, query_count, key_count):
    diag_span = query_count + key_count - 1
    head_count = grid.shape[0]
    widened = jnp.pad(grid, ((0, 0), (0, 0), (0, diag_span - 1 - key_count)))
    flat_rows = widened.reshape(head_count, query_count * (diag_span - 1))
    flat_rows = jnp.pad(flat_rows, ((0, 0), (query_count - 1, 1)))
    return jnp.sum(flat_rows.reshape(head_count, query_count, diag_span), axis=1)[:, ::-1]


def block_scores(query_block, query_first, key_block, key_first, seq_lengths, table, seq_total):
    query_count = query_block.shape[1]
    key_count = key_block.shape[1]
    score_scale = query_block.shape[3] ** (-0.5)
    dot_scores = (
        jnp.einsum("bqhd,bkhd->bhqk", query_block, key_block, preferred_element_type=FLOAT)
        * score_scale
    )
    one_hot = distance_onehot(
        table.shape[0], query_first, key_first + key_count - 1, query_count, key_count, seq_total
    )
    per_distance = jnp.dot(one_hot, table, precision=HIGHEST).T
    scores = dot_scores + expand_diagonals(per_distance, query_count, key_count)[None]
    query_pos = query_first + jnp.arange(query_count, dtype=jnp.int32)
    key_pos = key_first + jnp.arange(key_count, dtype=jnp.int32)
    causal = (query_pos[:, None] >= key_pos[None, :])[None]
    allowed = causal & (key_pos[None, None, :] < seq_lengths[:, None, None])
    return (scores, allowed[:, None], one_hot)


def block_needed(query_first, query_count, key_first, seq_lengths):
    return (key_first <= query_first + query_count - 1) & (key_first < jnp.max(seq_lengths))


def forward_step(
    running, key_block, value_block, key_first, queries, query_first, seq_lengths, table, seq_total
):
    row_peak, row_total, row_accum = running
    scores, allowed, one_hot = block_scores(
        queries, query_first, key_block, key_first, seq_lengths, table, seq_total
    )
    new_peak = jnp.maximum(row_peak, jnp.max(jnp.where(allowed, scores, NEGATIVE), axis=-1))
    weights = jnp.where(allowed, jnp.exp(scores - new_peak[..., None]), 0.0)
    factor = jnp.exp(row_peak - new_peak)
    row_total = row_total * factor + jnp.sum(weights, axis=-1)
    update = jnp.einsum(
        "bhqk,bkhd->bqhd", weights.astype(BFLOAT), value_block, preferred_element_type=FLOAT
    )
    row_accum = row_accum * jnp.transpose(factor, (0, 2, 1))[..., None] + update
    return (new_peak, row_total, row_accum)


def pair_grads(
    query_block,
    grad_out_block,
    log_block,
    delta_block,
    query_first,
    key_block,
    value_block,
    key_first,
    seq_lengths,
    table,
    seq_total,
):
    scores, allowed, one_hot = block_scores(
        query_block, query_first, key_block, key_first, seq_lengths, table, seq_total
    )
    weights = jnp.where(allowed, jnp.exp(scores - log_block[..., None]), 0.0)
    grad_weights = jnp.einsum(
        "bqhd,bkhd->bhqk", grad_out_block, value_block, preferred_element_type=FLOAT
    )
    grad_scores = (weights * (grad_weights - delta_block[..., None])).astype(BFLOAT)
    score_scale = query_block.shape[3] ** (-0.5)
    grad_query = (
        jnp.einsum("bhqk,bkhd->bqhd", grad_scores, key_block, preferred_element_type=FLOAT)
        * score_scale
    )
    grad_key = (
        jnp.einsum("bhqk,bqhd->bkhd", grad_scores, query_block, preferred_element_type=FLOAT)
        * score_scale
    )
    grad_value = jnp.einsum(
        "bhqk,bqhd->bkhd", weights.astype(BFLOAT), grad_out_block, preferred_element_type=FLOAT
    )
    per_distance = sum_diagonals(
        jnp.sum(grad_scores.astype(FLOAT), axis=0), query_block.shape[1], key_block.shape[1]
    )
    grad_table = jnp.dot(one_hot.T, per_distance.T, precision=HIGHEST)
    return (grad_query, grad_key, grad_value, grad_table)


def over_blocks(step_fn, running, members, block_rows):
    rows_in = members[0].shape[1]
    block_count = rows_in // block_rows
    stacked = tuple(
        (
            jnp.moveaxis(
                member.reshape((member.shape[0], block_count, block_rows) + member.shape[2:]), 1, 0
            )
            for member in members
        )
    )

    def scan_step(carried, scanned):
        block_number, blocks = scanned
        return (step_fn(carried, blocks, block_number * block_rows), None)

    result, unused = lax.scan(
        scan_step, running, (jnp.arange(block_count, dtype=jnp.int32), stacked)
    )
    return result


def keep_state(state):
    return state


def attend_forward(
    inputs, seq_lengths, norm_gain, norm_shift, weight_in, weight_out, table, seq_count
):
    normed = layer_norm(inputs, norm_gain, norm_shift).astype(BFLOAT)
    projected = dense(normed, weight_in).astype(BFLOAT)
    model_width = normed.shape[1]
    head_count = table.shape[1]
    head_dim = model_width // head_count
    local_frames = inputs.shape[0] // seq_count
    queries = projected[:, :model_width].reshape(seq_count, local_frames, head_count, head_dim)
    key_rows = projected[:, model_width : 2 * model_width].reshape(
        seq_count, local_frames, model_width
    )
    value_rows = projected[:, 2 * model_width :].reshape(seq_count, local_frames, model_width)
    seq_total = local_frames * lax.axis_size("tm")
    query_first = lax.axis_index("tm") * local_frames
    start_state = (
        jnp.full((seq_count, head_count, local_frames), NEGATIVE, FLOAT),
        jnp.zeros((seq_count, head_count, local_frames), FLOAT),
        jnp.zeros((seq_count, local_frames, head_count, head_dim), FLOAT),
    )

    def block_step(carried, blocks, block_first):

        def work_block(state):
            key_block = blocks[0].reshape(seq_count, -1, head_count, head_dim)
            value_block = blocks[1].reshape(seq_count, -1, head_count, head_dim)
            return forward_step(
                state,
                key_block,
                value_block,
                block_first,
                queries,
                query_first,
                seq_lengths,
                table,
                seq_total,
            )

        needed = block_needed(query_first, local_frames, block_first, seq_lengths)
        return lax.cond(needed, work_block, keep_state, carried)

    row_peak, row_total, row_accum = over_blocks(
        block_step,
        start_state,
        (
            lax.all_gather(key_rows, "tm", axis=1, tiled=True),
            lax.all_gather(value_rows, "tm", axis=1, tiled=True),
        ),
        local_frames,
    )
    attended = row_accum / jnp.transpose(row_total, (0, 2, 1))[..., None]
    log_total = row_peak + jnp.log(row_total)
    attended_low = attended.reshape(-1, model_width).astype(BFLOAT)
    branch = dense(attended_low, weight_out)
    return (branch, (normed, queries, key_rows, value_rows, attended, log_total, attended_low))


def attend_backward(
    inputs,
    seq_lengths,
    norm_gain,
    norm_shift,
    weight_in,
    weight_out,
    table,
    seq_count,
    stored,
    grad_branch,
):
    normed, queries, key_rows, value_rows, attended, log_total, attended_low = stored
    seq_count, local_frames, head_count, head_dim = queries.shape
    model_width = head_count * head_dim
    time_parts = lax.axis_size("tm")
    time_index = lax.axis_index("tm")
    seq_total = local_frames * time_parts
    query_first = time_index * local_frames
    grad_rounded = grad_branch.astype(BFLOAT)
    grad_out_weight = weight_grad(attended_low, grad_rounded)
    grad_attended = input_grad(grad_rounded, weight_out).astype(BFLOAT).reshape(attended.shape)
    row_delta = jnp.transpose(jnp.sum(grad_attended.astype(FLOAT) * attended, axis=-1), (0, 2, 1))
    zero_rows = jnp.zeros((seq_count, local_frames, head_count, head_dim), FLOAT)
    zero_table = jnp.zeros(table.shape, FLOAT)

    def visit_turn(turn_index, loop_state):
        key_block, value_block, grad_keys, grad_values, grad_query, grad_table = loop_state
        source_first = (time_index - turn_index) % time_parts * local_frames

        def add_terms(sums_in):
            pair_terms = pair_grads(
                queries,
                grad_attended,
                log_total,
                row_delta,
                query_first,
                key_block.reshape(seq_count, local_frames, head_count, head_dim),
                value_block.reshape(seq_count, local_frames, head_count, head_dim),
                source_first,
                seq_lengths,
                table,
                seq_total,
            )
            return (
                sums_in[0] + pair_terms[0],
                sums_in[1] + pair_terms[1],
                sums_in[2] + pair_terms[2],
                sums_in[3] + pair_terms[3],
            )

        needed = block_needed(query_first, local_frames, source_first, seq_lengths)
        grad_query, grad_keys, grad_values, grad_table = lax.cond(
            needed, add_terms, keep_state, (grad_query, grad_keys, grad_values, grad_table)
        )
        key_block, value_block = passed_along((key_block, value_block), "tm", 1)
        grad_keys, grad_values = (
            from_behind(grad_keys.astype(jnp.bfloat16), "tm", 1).astype(grad_keys.dtype),
            from_behind(grad_values.astype(jnp.bfloat16), "tm", 1).astype(grad_values.dtype),
        )
        return (key_block, value_block, grad_keys, grad_values, grad_query, grad_table)

    final_state = lax.fori_loop(
        0,
        time_parts,
        visit_turn,
        (key_rows, value_rows, zero_rows, zero_rows, zero_rows, zero_table),
    )
    grad_keys, grad_values, grad_query, grad_table = (
        final_state[2],
        final_state[3],
        final_state[4],
        final_state[5],
    )
    grad_projected = jnp.concatenate(
        [
            grad_query.reshape(-1, model_width),
            grad_keys.reshape(-1, model_width),
            grad_values.reshape(-1, model_width),
        ],
        axis=1,
    ).astype(BFLOAT)
    grad_in_weight = weight_grad(normed, grad_projected)
    grad_normed = input_grad(grad_projected, weight_in)
    grad_inputs, grad_gain, grad_shift = norm_backward(inputs, norm_gain, norm_shift, grad_normed)
    return (grad_inputs, (grad_gain, grad_shift, grad_in_weight, grad_out_weight, grad_table))


def gate_units(projected, valid_rows):
    channels = projected.shape[1] // 2
    return projected[:, :channels] * jax.nn.sigmoid(projected[:, channels:]) * valid_rows


def inner_apply(values, gain_in, shift_in):
    return jax.nn.silu(layer_norm(values, gain_in, shift_in))


def convolve_forward(
    inputs,
    seq_lengths,
    norm_gain,
    norm_shift,
    weight_in,
    depth,
    inner_gain,
    inner_shift,
    weight_out,
    seq_count,
):
    normed = layer_norm(inputs, norm_gain, norm_shift).astype(BFLOAT)
    projected = dense(normed, weight_in)
    channels = weight_out.shape[0]
    local_frames = inputs.shape[0] // seq_count
    kernel = depth.shape[1]
    positions = lax.axis_index("tm") * local_frames + jnp.arange(local_frames, dtype=jnp.int32)
    valid_rows = (positions[None, :] < seq_lengths[:, None]).astype(FLOAT).reshape(-1, 1)
    gated_units = (
        gate_units(projected, valid_rows).astype(BFLOAT).reshape(seq_count, local_frames, channels)
    )
    history = passed_along(gated_units[:, local_frames - (kernel - 1) :, :], "tm", 1)
    extended = jnp.concatenate([history, gated_units], axis=1).astype(FLOAT)
    filtered = depth[:, 0] * extended[:, 0:local_frames]
    for tap_index in range(1, kernel):
        filtered = (
            filtered + depth[:, tap_index] * extended[:, tap_index : tap_index + local_frames]
        )
    active = inner_apply(filtered, inner_gain, inner_shift).astype(BFLOAT).reshape(-1, channels)
    branch = dense(active, weight_out)
    return (branch, (normed, projected, valid_rows, extended, filtered, active))


def convolve_backward(
    inputs,
    norm_gain,
    norm_shift,
    weight_in,
    depth,
    inner_gain,
    inner_shift,
    weight_out,
    stored,
    grad_branch,
):
    normed, projected, valid_rows, extended, filtered, active = stored
    local_frames = filtered.shape[1]
    channels = filtered.shape[2]
    kernel = depth.shape[1]
    grad_rounded = grad_branch.astype(BFLOAT)
    grad_out_weight = weight_grad(active, grad_rounded)
    grad_active = input_grad(grad_rounded, weight_out).reshape(filtered.shape)
    unused, pullback = jax.vjp(inner_apply, filtered, inner_gain, inner_shift)
    grad_filtered, grad_inner_gain, grad_inner_shift = pullback(grad_active)
    tap_terms = [
        jnp.sum(grad_filtered * extended[:, tap_index : tap_index + local_frames], axis=(0, 1))
        for tap_index in range(kernel)
    ]
    grad_depth = jnp.stack(tap_terms, axis=1)
    grad_extended = jnp.pad(depth[:, 0] * grad_filtered, ((0, 0), (0, kernel - 1), (0, 0)))
    for tap_index in range(1, kernel):
        grad_extended = grad_extended + jnp.pad(
            depth[:, tap_index] * grad_filtered,
            ((0, 0), (tap_index, kernel - 1 - tap_index), (0, 0)),
        )
    returned = passed_along(grad_extended[:, : kernel - 1].astype(jnp.bfloat16), "tm", -1).astype(
        jnp.float32
    )
    grad_units = grad_extended[:, kernel - 1 :] + jnp.pad(
        returned, ((0, 0), (local_frames - (kernel - 1), 0), (0, 0))
    )
    unused_gate, gate_pull = jax.vjp(lambda values: gate_units(values, valid_rows), projected)
    grad_projected = gate_pull(grad_units.reshape(-1, channels))[0].astype(BFLOAT)
    grad_in_weight = weight_grad(normed, grad_projected)
    grad_normed = input_grad(grad_projected, weight_in)
    grad_inputs, grad_gain, grad_shift = norm_backward(inputs, norm_gain, norm_shift, grad_normed)
    return (
        grad_inputs,
        (
            grad_gain,
            grad_shift,
            grad_in_weight,
            grad_depth,
            grad_inner_gain,
            grad_inner_shift,
            grad_out_weight,
        ),
    )


def body(
    frames,
    cotangent,
    lengths,
    early_gain,
    early_shift,
    early_up,
    early_down,
    attend_gain,
    attend_shift,
    attend_input,
    attend_output,
    distance_bias,
    convolve_gain,
    convolve_shift,
    convolve_input,
    depthwise,
    inner_gain,
    inner_shift,
    convolve_output,
    late_gain,
    late_shift,
    late_up,
    late_down,
    final_gain,
    final_shift,
):
    seq_count, local_frames, model_width = frames.shape
    early_norm = (early_gain.astype(FLOAT), early_shift.astype(FLOAT))
    attend_norm = (attend_gain.astype(FLOAT), attend_shift.astype(FLOAT))
    convolve_norm = (convolve_gain.astype(FLOAT), convolve_shift.astype(FLOAT))
    inner_norm = (inner_gain.astype(FLOAT), inner_shift.astype(FLOAT))
    late_norm = (late_gain.astype(FLOAT), late_shift.astype(FLOAT))
    final_norm = (final_gain.astype(FLOAT), final_shift.astype(FLOAT))
    table_float = distance_bias.astype(FLOAT)
    depth_float = depthwise.astype(FLOAT)
    state_zero = frames.reshape(-1, model_width).astype(FLOAT)
    early_branch, early_kept = ffn_forward(
        state_zero, early_norm[0], early_norm[1], early_up, early_down
    )
    state_one = state_zero + 0.5 * early_branch
    attend_branch, attend_kept = attend_forward(
        state_one,
        lengths,
        attend_norm[0],
        attend_norm[1],
        attend_input,
        attend_output,
        table_float,
        seq_count,
    )
    state_two = state_one + attend_branch
    conv_branch, conv_kept = convolve_forward(
        state_two,
        lengths,
        convolve_norm[0],
        convolve_norm[1],
        convolve_input,
        depth_float,
        inner_norm[0],
        inner_norm[1],
        convolve_output,
        seq_count,
    )
    state_three = state_two + conv_branch
    late_branch, late_kept = ffn_forward(
        state_three, late_norm[0], late_norm[1], late_up, late_down
    )
    state_four = state_three + 0.5 * late_branch
    layer_out, final_pull = jax.vjp(layer_norm, state_four, final_norm[0], final_norm[1])
    grad_four, grad_final_gain, grad_final_shift = final_pull(
        cotangent.reshape(-1, model_width).astype(FLOAT)
    )
    grad_late_in, late_grads = ffn_backward(
        state_three, late_norm[0], late_norm[1], late_up, late_down, late_kept, 0.5 * grad_four
    )
    grad_three = grad_four + grad_late_in
    grad_conv_in, conv_grads = convolve_backward(
        state_two,
        convolve_norm[0],
        convolve_norm[1],
        convolve_input,
        depth_float,
        inner_norm[0],
        inner_norm[1],
        convolve_output,
        conv_kept,
        grad_three,
    )
    grad_two = grad_three + grad_conv_in
    grad_attend_in, attend_grads = attend_backward(
        state_one,
        lengths,
        attend_norm[0],
        attend_norm[1],
        attend_input,
        attend_output,
        table_float,
        seq_count,
        attend_kept,
        grad_two,
    )
    grad_one = grad_two + grad_attend_in
    grad_early_in, early_grads = ffn_backward(
        state_zero, early_norm[0], early_norm[1], early_up, early_down, early_kept, 0.5 * grad_one
    )
    grad_zero = grad_one + grad_early_in
    gradient_list = (
        early_grads[0],
        early_grads[1],
        early_grads[2],
        early_grads[3],
        attend_grads[0],
        attend_grads[1],
        attend_grads[2],
        attend_grads[3],
        attend_grads[4],
        conv_grads[0],
        conv_grads[1],
        conv_grads[2],
        conv_grads[3],
        conv_grads[4],
        conv_grads[5],
        conv_grads[6],
        late_grads[0],
        late_grads[1],
        late_grads[2],
        late_grads[3],
        grad_final_gain,
        grad_final_shift,
    )
    reduced = (
        lax.psum_scatter(
            gradient_list[0].astype(jnp.bfloat16), "rows", scatter_dimension=0, tiled=True
        ).astype(jnp.float32),
        lax.psum_scatter(
            gradient_list[1].astype(jnp.bfloat16), "rows", scatter_dimension=0, tiled=True
        ).astype(jnp.float32),
        lax.psum_scatter(
            gradient_list[2].astype(jnp.bfloat16), "rows", scatter_dimension=0, tiled=True
        ).astype(jnp.float32),
        lax.psum_scatter(
            gradient_list[3].astype(jnp.bfloat16), "rows", scatter_dimension=0, tiled=True
        ).astype(jnp.float32),
        lax.psum_scatter(
            gradient_list[4].astype(jnp.bfloat16), "rows", scatter_dimension=0, tiled=True
        ).astype(jnp.float32),
        lax.psum_scatter(
            gradient_list[5].astype(jnp.bfloat16), "rows", scatter_dimension=0, tiled=True
        ).astype(jnp.float32),
        lax.psum_scatter(
            gradient_list[6].astype(jnp.bfloat16), "rows", scatter_dimension=0, tiled=True
        ).astype(jnp.float32),
        lax.psum_scatter(
            gradient_list[7].astype(jnp.bfloat16), "rows", scatter_dimension=0, tiled=True
        ).astype(jnp.float32),
        lax.psum_scatter(
            gradient_list[8].astype(jnp.bfloat16), "rows", scatter_dimension=0, tiled=True
        ).astype(jnp.float32),
        lax.psum_scatter(
            gradient_list[9].astype(jnp.bfloat16), "rows", scatter_dimension=0, tiled=True
        ).astype(jnp.float32),
        lax.psum_scatter(
            gradient_list[10].astype(jnp.bfloat16), "rows", scatter_dimension=0, tiled=True
        ).astype(jnp.float32),
        lax.psum_scatter(
            gradient_list[11].astype(jnp.bfloat16), "rows", scatter_dimension=0, tiled=True
        ).astype(jnp.float32),
        lax.psum_scatter(
            gradient_list[12].astype(jnp.bfloat16), "rows", scatter_dimension=0, tiled=True
        ).astype(jnp.float32),
        lax.psum_scatter(
            gradient_list[13].astype(jnp.bfloat16), "rows", scatter_dimension=0, tiled=True
        ).astype(jnp.float32),
        lax.psum_scatter(
            gradient_list[14].astype(jnp.bfloat16), "rows", scatter_dimension=0, tiled=True
        ).astype(jnp.float32),
        lax.psum_scatter(
            gradient_list[15].astype(jnp.bfloat16), "rows", scatter_dimension=0, tiled=True
        ).astype(jnp.float32),
        lax.psum_scatter(
            gradient_list[16].astype(jnp.bfloat16), "rows", scatter_dimension=0, tiled=True
        ).astype(jnp.float32),
        lax.psum_scatter(
            gradient_list[17].astype(jnp.bfloat16), "rows", scatter_dimension=0, tiled=True
        ).astype(jnp.float32),
        lax.psum_scatter(
            gradient_list[18].astype(jnp.bfloat16), "rows", scatter_dimension=0, tiled=True
        ).astype(jnp.float32),
        lax.psum_scatter(
            gradient_list[19].astype(jnp.bfloat16), "rows", scatter_dimension=0, tiled=True
        ).astype(jnp.float32),
        lax.psum_scatter(
            gradient_list[20].astype(jnp.bfloat16), "rows", scatter_dimension=0, tiled=True
        ).astype(jnp.float32),
        lax.psum_scatter(
            gradient_list[21].astype(jnp.bfloat16), "rows", scatter_dimension=0, tiled=True
        ).astype(jnp.float32),
    )
    summed = (
        lax.psum(reduced[0].astype(jnp.bfloat16), "tm").astype(jnp.float32),
        lax.psum(reduced[1].astype(jnp.bfloat16), "tm").astype(jnp.float32),
        lax.psum(reduced[2].astype(jnp.bfloat16), "tm").astype(jnp.float32),
        lax.psum(reduced[3].astype(jnp.bfloat16), "tm").astype(jnp.float32),
        lax.psum(reduced[4].astype(jnp.bfloat16), "tm").astype(jnp.float32),
        lax.psum(reduced[5].astype(jnp.bfloat16), "tm").astype(jnp.float32),
        lax.psum(reduced[6].astype(jnp.bfloat16), "tm").astype(jnp.float32),
        lax.psum(reduced[7].astype(jnp.bfloat16), "tm").astype(jnp.float32),
        lax.psum(reduced[8].astype(jnp.bfloat16), "tm").astype(jnp.float32),
        lax.psum(reduced[9].astype(jnp.bfloat16), "tm").astype(jnp.float32),
        lax.psum(reduced[10].astype(jnp.bfloat16), "tm").astype(jnp.float32),
        lax.psum(reduced[11].astype(jnp.bfloat16), "tm").astype(jnp.float32),
        lax.psum(reduced[12].astype(jnp.bfloat16), "tm").astype(jnp.float32),
        lax.psum(reduced[13].astype(jnp.bfloat16), "tm").astype(jnp.float32),
        lax.psum(reduced[14].astype(jnp.bfloat16), "tm").astype(jnp.float32),
        lax.psum(reduced[15].astype(jnp.bfloat16), "tm").astype(jnp.float32),
        lax.psum(reduced[16].astype(jnp.bfloat16), "tm").astype(jnp.float32),
        lax.psum(reduced[17].astype(jnp.bfloat16), "tm").astype(jnp.float32),
        lax.psum(reduced[18].astype(jnp.bfloat16), "tm").astype(jnp.float32),
        lax.psum(reduced[19].astype(jnp.bfloat16), "tm").astype(jnp.float32),
        lax.psum(reduced[20].astype(jnp.bfloat16), "tm").astype(jnp.float32),
        lax.psum(reduced[21].astype(jnp.bfloat16), "tm").astype(jnp.float32),
    )
    out_rows = layer_out.astype(BFLOAT).reshape(seq_count, local_frames, model_width)
    grad_rows_out = grad_zero.astype(BFLOAT).reshape(seq_count, local_frames, model_width)
    return (
        out_rows,
        grad_rows_out,
        summed[0],
        summed[1],
        summed[2],
        summed[3],
        summed[4],
        summed[5],
        summed[6],
        summed[7],
        summed[8],
        summed[9],
        summed[10],
        summed[11],
        summed[12],
        summed[13],
        summed[14],
        summed[15],
        summed[16],
        summed[17],
        summed[18],
        summed[19],
        summed[20],
        summed[21],
    )


def solution(mesh):
    placed = (
        P("rows", "tm", None),
        P("rows", "tm", None),
        P("rows"),
        P(),
        P(),
        P(),
        P(),
        P(),
        P(),
        P(),
        P(),
        P(),
        P(),
        P(),
        P(),
        P(),
        P(),
        P(),
        P(),
        P(),
        P(),
        P(),
        P(),
        P(),
        P(),
    )
    return jax.shard_map(
        body,
        mesh=mesh,
        in_specs=placed,
        out_specs=(
            P("rows", "tm", None),
            P("rows", "tm", None),
            P("rows"),
            P("rows"),
            P("rows", None),
            P("rows", None),
            P("rows"),
            P("rows"),
            P("rows", None),
            P("rows", None),
            P("rows", None),
            P("rows"),
            P("rows"),
            P("rows", None),
            P("rows", None),
            P("rows"),
            P("rows"),
            P("rows", None),
            P("rows"),
            P("rows"),
            P("rows", None),
            P("rows", None),
            P("rows"),
            P("rows"),
        ),
        check_vma=False,
    )
```

profile of v0, /device:TPU:0, one launch (start us, length us, event | category | flops | bytes accessed | tf_op | source)
XLA Modules:
  0.0 1743.1 jit_solution(8302059127786084653)
XLA Ops:
  15.1 6.9 multiply_convert_fusion.2
  35.1 39.8 %all-gather.5.cloned.1.call-done = bf16[2,1536,512]{2,1,0:T(8,128)(2,1)} async-done(((bf16[2,384,512]{2,1,0:T(8,128)(2,1)}), bf16[2,1536,512]{2,1,0:T(8,128)(2,1)}) %all-gather.5.cloned.1.call-update) | async-done | bytes 3145744 | tf_op jit(solution)/shard_map/all_gather | solution.py:257
  79.6 41.2 %all-gather.3.cloned.1.call-done = bf16[2,1536,512]{2,1,0:T(8,128)(2,1)} async-done(((bf16[2,384,512]{2,1,0:T(8,128)(2,1)}), bf16[2,1536,512]{2,1,0:T(8,128)(2,1)}) %all-gather.3.cloned.1.call-update) | async-done | bytes 3145744 | tf_op jit(solution)/shard_map/all_gather | solution.py:256
  126.8 90.7 %while.44 = (s32[]{:T(128)}, f32[2,8,384]{2,1,0:T(8,128)S(1)}, f32[2,8,384]{2,1,0:T(8,128)S(1)}, f32[2,384,8,64]{1,3,2,0:T(8,128)}, s32[4]{0:T(128)S(1)}, /*inde...) while((s32[]{:T(128)}, f32[2,8,384]{2,1,0:T(8,128)S(1)}, ...), condition=%wide.region_11.12_spmd.clone, body=%wide.region_5.11_spmd.sunk.clone.sunk | while | flops 640711552 | bytes 210233840 | solution.py:200
  128.8 82.6 %conditional.9 = ((f32[2,8,384]{2,1,0:T(8,128)S(1)}, f32[2,8,384]{2,1,0:T(8,128)S(1)}, f32[2,384,8,64]{1,3,2,0:T(8,128)})) conditional(s32[]{:T(128)} %convert_element_type.643, (f32[2,8,384]{2,1,0:T(8,128)S(1)}, f32[2,8,384]{2,1,0:T(8,128)S(1)}, f32[2,384,8,64]{1,3,2,0:T(8,128)}) %tuple.208, (s32[]{:T(128)}, s32[]{:T(128)}, s32[2]{0:T(128)S(1)}, ...), branch_computations={%region_6.6_spmd, %region_7.10_spmd.clone} | conditional | flops 640711552 | bytes 210233536 | solution.py:250
  137.9 10.7 reshape.597
  148.7 10.0 tile.21
  158.6 9.4 slice.205
  168.1 8.0 reshape.599
  176.1 13.4 reshape.593
  189.5 4.9 slice.206
  194.4 6.1 copy.135
  200.5 4.7 select_reduce_fusion
  229.0 86.0 %collective-permute-start.4 = (bf16[2,14,1024]{2,1,0:T(8,128)(2,1)S(1)}, bf16[2,14,1024]{2,1,0:T(8,128)(2,1)S(1)}, u32[]{:S(2)}, u32[]{:S(2)}) collective-permute-start(bf16[2,14,1024]{2,1,0:T(8,128)(2,1)S(1)} %slice.215), channel_id=1, source_target_pairs={{0,1},{1,2},{2,3},{4,5},{5,6},{6,7},{8,9},{9,10},{10,11},{12,13},{... | collective-permute-start | bytes 172040 | tf_op jit(solution)/shard_map/ppermute | solution.py:16
  319.0 26.7 %fusion.75 = (f32[2,384]{1,0:T(2,128)S(1)}, f32[2,384,1024]{2,1,0:T(8,128)}) fusion(f32[2,398,1024]{2,1,0:T(8,128)} %maximum_convert_fusion, f32[1024]{0:T(1024)S(1)} %bitcast.245, f32[1024]{0:T(1024)S(1)} %bitcast.243, f32[1024]{0:T(1024)S(1)} %bitcast.241, f32[1024]{0:T(1024)S(1)} %bitcast.239, f32[1024]{0:T(1024)S(1)} %bitcast.237, ...), kind=kLoop, calls=%fused_computation.235 | loop fusion | flops 23592192 | bytes 50396160 | tf_op jit(solution)/shard_map/reduce_sum | solution.py:33
  372.0 8.7 multiply_reduce_fusion.1
  380.8 16.8 broadcast_multiply_fusion.14
  397.6 19.9 %pad_add_fusion = f32[2,398,1024]{2,1,0:T(8,128)} fusion(f32[2,384,1024]{2,1,0:T(8,128)} %get-tuple-element.1277, f32[2,384,1024]{2,1,0:T(8,128)} %get-tuple-element.1278, f32[2,384,1024]{2,1,0:T(8,128)} %get-tuple-element.1279, f32[2,384,1024]{2,1,0:T(8,128)} %get-tuple-element.1280, f32[2,384,1024]{2,1,0:T(8,128)} %get-tuple-element.1281, ...), kind=kLoop, calls=%fused_computation.67 | loop fusion | flops 11411456 | bytes 50446336 | tf_op jit(solution)/shard_map/add | solution.py:427
  419.7 86.9 %collective-permute-done.5 = bf16[2,14,1024]{2,1,0:T(8,128)(2,1)S(1)} collective-permute-done((bf16[2,14,1024]{2,1,0:T(8,128)(2,1)S(1)}, bf16[2,14,1024]{2,1,0:T(8,128)(2,1)S(1)}, u32[]{:S(2)}, u32[]{:S(2)}) %collective-permute-start.5) | collective-permute-done | bytes 57376 | tf_op jit(solution)/shard_map/ppermute | solution.py:16
  539.9 829.8 %while.45 = (s32[]{:T(128)}, bf16[2,384,512]{1,2,0:T(8,128)(2,1)S(1)}, bf16[2,384,512]{1,2,0:T(8,128)(2,1)S(1)}, f32[2,384,8,64]{1,3,2,0:T(8,128)}, f32[2,384,8,...) while((s32[]{:T(128)}, ...), condition=%wide.region_35.36_spmd.clone.clone, body=%wide.region_29.35_spmd.sunk.clone.clone.sunk | while | flops 1553753216 | bytes 369934144 | solution.py:330
  544.6 140.2 %conditional.10 = ((f32[2,384,8,64]{1,3,2,0:T(8,128)}, f32[2,384,8,64]{1,3,2,0:T(8,128)}, f32[2,384,8,64]{1,3,2,0:T(8,128)S(1)}, f32[32,8]{0,1:T(8,128)S(1)})) conditional(s32[]{:T(128)} %convert_element_type.644, (f32[2,384,8,64]{1,3,2,0:T(8,128)}, f32[2,384,8,64]{1,3,2,0:T(8,128)}, f32[2,384,8,64]{1,3,2,0:T(8,128)S(1)}, ...), branch_computations={%region_30.30_spmd, %region_31.34_spmd.clone} | conditional | flops 1551393920 | bytes 319601792 | solution.py:320
  550.9 10.7 reshape.601
  561.7 10.0 tile.23
  571.6 9.4 slice.207
  581.1 8.0 reshape.603
  589.1 13.4 reshape.594
  610.5 6.5 convert_reduce_fusion.1
  618.2 5.2 bitcast_add_fusion.4
  627.8 10.8 reshape.605
  638.6 10.2 reshape.595
  648.8 9.5 pad.101
  658.3 7.9 reshape.607
  666.2 13.6 reshape.596
  696.8 10.8 collective-permute-done.3
  710.0 14.4 collective-permute-done.2
  726.8 14.4 collective-permute-done
  741.3 13.5 collective-permute-done.1
  760.3 142.5 %collective-permute-start.3 = (bf16[2,384,8,64]{1,3,2,0:T(8,128)(2,1)}, bf16[2,384,8,64]{1,3,2,0:T(8,128)(2,1)}, u32[]{:S(2)}, u32[]{:S(2)}) collective-permute-start(bf16[2,384,8,64]{1,3,2,0:T(8,128)(2,1)} %convert_element_type.647), channel_id=1, source_target_pairs={{0,1},{1,2},{2,3},{3,0},{4,5},{5,6},{6,7},{7,4},{8,9},{9,10},{10,1... | collective-permute-start | bytes 2359304 | tf_op jit(solution)/shard_map/while/body/eval_jaxpr/ppermute | solution.py:22
  911.0 10.6 collective-permute-done.3
  924.0 13.9 collective-permute-done.2
  940.3 14.4 collective-permute-done
  954.8 12.6 collective-permute-done.1
  976.3 143.4 %collective-permute-start.2 = (bf16[2,384,8,64]{1,3,2,0:T(8,128)(2,1)}, bf16[2,384,8,64]{1,3,2,0:T(8,128)(2,1)}, u32[]{:S(2)}, u32[]{:S(2)}) collective-permute-start(bf16[2,384,8,64]{1,3,2,0:T(8,128)(2,1)} %convert_element_type.645), channel_id=1, source_target_pairs={{0,1},{1,2},{2,3},{3,0},{4,5},{5,6},{6,7},{7,4},{8,9},{9,10},{10,1... | collective-permute-start | bytes 2359304 | tf_op jit(solution)/shard_map/while/body/eval_jaxpr/ppermute | solution.py:22
  1124.3 10.6 collective-permute-done.3
  1137.3 9.5 collective-permute-done.2
  1149.3 5.6 collective-permute-done
  1154.9 11.2 collective-permute-done.1
  1171.5 16.1 collective-permute-start.3
  1192.0 141.4 %collective-permute-start = (bf16[2,384,512]{1,2,0:T(8,128)(2,1)}, bf16[2,384,512]{1,2,0:T(8,128)(2,1)S(1)}, u32[]{:S(2)}, u32[]{:S(2)}) collective-permute-start(bf16[2,384,512]{1,2,0:T(8,128)(2,1)} %copy.176), channel_id=1, source_target_pairs={{0,1},{1,2},{2,3},{4,5},{5,6},{6,7},{8,9},{9,10},{10,11},{12,13},{... | collective-permute-start | bytes 2359304 | tf_op jit(solution)/shard_map/while/body/eval_jaxpr/ppermute | solution.py:16
  1336.0 11.2 collective-permute-done.3
  1349.7 8.6 collective-permute-done.2
  1380.6 5.6 convolution_convert_fusion.1
  1386.4 5.8 convolution_convert_fusion.2
  1392.3 6.2 convolution_convert_fusion.3
  1409.7 7.0 fusion.26
  1426.2 16.1 reduce-scatter.16.cloned.1.call-done
  1442.4 35.9 %reduce-scatter.26.cloned.1.call-done = bf16[256,512]{1,0:T(8,128)(2,1)} async-done(((bf16[2048,512]{1,0:T(8,128)(2,1)}), bf16[256,512]{1,0:T(8,128)(2,1)}) %reduce-scatter.26.cloned.1.call-update) | async-done | bytes 262160 | tf_op jit(solution)/shard_map/reduce_scatter | solution.py:645
  1478.3 36.7 %reduce-scatter.24.cloned.1.call-done = bf16[64,2048]{1,0:T(8,128)(2,1)} async-done(((bf16[512,2048]{1,0:T(8,128)(2,1)}), bf16[64,2048]{1,0:T(8,128)(2,1)}) %reduce-scatter.24.cloned.1.call-update) | async-done | bytes 262160 | tf_op jit(solution)/shard_map/reduce_scatter | solution.py:642
  1515.0 36.9 %reduce-scatter.20.cloned.1.call-done = bf16[64,2048]{1,0:T(8,128)(2,1)} async-done(((bf16[512,2048]{1,0:T(8,128)(2,1)}), bf16[64,2048]{1,0:T(8,128)(2,1)}) %reduce-scatter.20.cloned.1.call-update) | async-done | bytes 262160 | tf_op jit(solution)/shard_map/reduce_scatter | solution.py:621
  1551.9 36.9 %reduce-scatter.14.cloned.1.call-done = bf16[256,512]{1,0:T(8,128)(2,1)} async-done(((bf16[2048,512]{1,0:T(8,128)(2,1)}), bf16[256,512]{1,0:T(8,128)(2,1)}) %reduce-scatter.14.cloned.1.call-update) | async-done | bytes 262160 | tf_op jit(solution)/shard_map/reduce_scatter | solution.py:597
  1588.8 36.5 %reduce-scatter.12.cloned.1.call-done = bf16[64,2048]{1,0:T(8,128)(2,1)} async-done(((bf16[512,2048]{1,0:T(8,128)(2,1)}), bf16[64,2048]{1,0:T(8,128)(2,1)}) %reduce-scatter.12.cloned.1.call-update) | async-done | bytes 262160 | tf_op jit(solution)/shard_map/reduce_scatter | solution.py:594
  1632.0 27.1 %all-reduce.33 = (bf16[512]{0:T(512)(128)(2,1)S(1)}, bf16[512]{0:T(512)(128)(2,1)S(1)}, bf16[512]{0:T(512)(128)(2,1)S(1)}, bf16[512]{0:T(512)(128)(2,1)S(1)}, bf...) all-reduce(bf16[512]{0:T(512)(128)(2,1)S(1)} %get-tuple-element.114, ...), channel_id=2, replica_groups=mesh['rows'=8,'tm'=4] {'rows'}, use_global_device_ids=true, to_apply=%region_41.42.clone | all-reduce | flops 7424 | bytes 29696
  1664.2 16.2 all-reduce.34
  1687.7 36.3 %all-reduce.38.cloned.1.call-done = (bf16[64,2048]{1,0:T(8,128)(2,1)}, bf16[256,512]{1,0:T(8,128)(2,1)}, bf16[64,1536]{1,0:T(8,128)(2,1)}, bf16[64,512]{1,0:T(8,...) async-done(((bf16[64,2048]{1,0:T(8,128)(2,1)}, bf16[256,512]{1,0:T(8,128)(2,1)}, ...) | async-done | bytes 1703952 | tf_op jit(solution)/shard_map/psum | solution.py:658
  (573 shorter events, 284.6 us)
Async XLA Ops:
  7.2 344.0 %copy-start = (bf16[512,2048]{1,0:T(8,128)(2,1)S(1)}, bf16[512,2048]{1,0:T(8,128)(2,1)}, u32[]{:S(2)}) copy-start(bf16[512,2048]{1,0:T(8,128)(2,1)} %param.56) | copy-start | bytes 6291460
  7.2 67.7 %all-gather.5.cloned.1.call-start = ((), (), s32[]{:S(2)}) async-start(), calls=%async_computation.10 | async-start | bytes 3932160 | tf_op jit(solution)/shard_map/all_gather | solution.py:257
  10.2 11.8 copy-start.62
  10.9 11.1 copy-start.78
  11.6 13.5 copy-start.99
  12.3 12.8 copy-start.107
  13.0 9.0 copy-start.74
  15.1 6.9 copy-start.20
  28.1 92.7 %all-gather.3.cloned.1.call-start = ((), (), s32[]{:S(2)}) async-start(), calls=%async_computation.9 | async-start | bytes 3932160 | tf_op jit(solution)/shard_map/all_gather | solution.py:256
  28.8 1397.4 %reduce-scatter.18.cloned.1.call-start = ((), (), s32[]{:S(2)}) async-start(), calls=%async_computation.14 | async-start | bytes 589824 | tf_op jit(solution)/shard_map/reduce_scatter | solution.py:609
  222.8 292.8 %copy-start.16 = (f32[768,512]{1,0:T(8,128)}, f32[768,512]{1,0:T(8,128)S(1)}, u32[]{:S(2)}) copy-start(f32[768,512]{1,0:T(8,128)S(1)} %get-tuple-element.1315) | copy-start | bytes 4718596
  222.8 292.8 %copy-start.49 = (f32[768]{0:T(1024)}, f32[768]{0:T(1024)S(1)}, u32[]{:S(2)}) copy-start(f32[768]{0:T(1024)S(1)} %broadcast_multiply_fusion.17) | copy-start | bytes 9220
  224.4 291.2 %copy-start.53 = (f32[768]{0:T(1024)}, f32[768]{0:T(1024)S(1)}, u32[]{:S(2)}) copy-start(f32[768]{0:T(1024)S(1)} %fusion.57) | copy-start | bytes 9220
  226.3 88.6 %copy-start.57 = (bf16[1024,15]{0,1:T(8,128)(2,1)S(1)}, bf16[1024,15]{0,1:T(8,128)(2,1)}, u32[]{:S(2)}) copy-start(bf16[1024,15]{0,1:T(8,128)(2,1)} %param.50) | copy-start | bytes 92164
  226.3 88.7 %copy-start.111 = (bf16[512]{0:T(512)(128)(2,1)S(1)}, bf16[512]{0:T(512)(128)(2,1)}, u32[]{:S(2)}) copy-start(bf16[512]{0:T(512)(128)(2,1)} %param.54) | copy-start | bytes 3076
  226.3 88.7 %copy-start.112 = (bf16[512]{0:T(512)(128)(2,1)S(1)}, bf16[512]{0:T(512)(128)(2,1)}, u32[]{:S(2)}) copy-start(bf16[512]{0:T(512)(128)(2,1)} %param.55) | copy-start | bytes 3076
  226.3 88.7 %copy-start.113 = (bf16[512]{0:T(512)(128)(2,1)S(1)}, bf16[512]{0:T(512)(128)(2,1)}, u32[]{:S(2)}) copy-start(bf16[512]{0:T(512)(128)(2,1)} %param.58) | copy-start | bytes 3076
  226.3 88.7 %copy-start.114 = (bf16[512]{0:T(512)(128)(2,1)S(1)}, bf16[512]{0:T(512)(128)(2,1)}, u32[]{:S(2)}) copy-start(bf16[512]{0:T(512)(128)(2,1)} %param.59) | copy-start | bytes 3076
  226.4 88.7 %copy-start.105 = (bf16[1024]{0:T(1024)(128)(2,1)S(1)}, bf16[1024]{0:T(1024)(128)(2,1)}, u32[]{:S(2)}) copy-start(bf16[1024]{0:T(1024)(128)(2,1)} %param.51) | copy-start | bytes 6148
  226.4 88.8 %copy-start.106 = (bf16[1024]{0:T(1024)(128)(2,1)S(1)}, bf16[1024]{0:T(1024)(128)(2,1)}, u32[]{:S(2)}) copy-start(bf16[1024]{0:T(1024)(128)(2,1)} %param.52) | copy-start | bytes 6148
  229.0 87.9 %collective-permute-start.4 = (bf16[2,14,1024]{2,1,0:T(8,128)(2,1)S(1)}, bf16[2,14,1024]{2,1,0:T(8,128)(2,1)S(1)}, u32[]{:S(2)}, u32[]{:S(2)}) collective-permute-start(bf16[2,14,1024]{2,1,0:T(8,128)(2,1)S(1)} %slice.215), channel_id=1, source_target_pairs={{0,1},{1,2},{2,3},{4,5},{5,6},{6,7},{8,9},{9,10},{10,11},{12,13},{... | collective-permute-start | bytes 172040 | tf_op jit(solution)/shard_map/ppermute | solution.py:16
  315.0 50.1 %copy-start.60 = (f32[512]{0:T(512)}, f32[512]{0:T(512)S(1)}, u32[]{:S(2)}) copy-start(f32[512]{0:T(512)S(1)} %convert_element_type.453) | copy-start | bytes 6148
  315.1 36.1 %copy-start.69 = (f32[512]{0:T(512)}, f32[512]{0:T(512)S(1)}, u32[]{:S(2)}) copy-start(f32[512]{0:T(512)S(1)} %convert_element_type.454) | copy-start | bytes 6148
  350.8 14.4 copy-start.28
  350.8 14.4 copy-start.51
  351.2 14.0 copy-start.55
  358.9 6.9 copy-start.36
  358.9 7.0 copy-start.80
  418.4 88.2 %collective-permute-start.5 = (bf16[2,14,1024]{2,1,0:T(8,128)(2,1)S(1)}, bf16[2,14,1024]{2,1,0:T(8,128)(2,1)S(1)}, u32[]{:S(2)}, u32[]{:S(2)}) collective-permute-start(bf16[2,14,1024]{2,1,0:T(8,128)(2,1)S(1)} %slice.297), channel_id=1, source_target_pairs={{1,0},{2,1},{3,2},{5,4},{6,5},{7,6},{9,8},{10,9},{11,10},{13,12},{... | collective-permute-start | bytes 172040 | tf_op jit(solution)/shard_map/ppermute | solution.py:16
  518.9 907.4 %reduce-scatter.22.cloned.1.call-start = ((), (), s32[]{:S(2)}) async-start(), calls=%async_computation.16 | async-start | bytes 1179648 | tf_op jit(solution)/shard_map/reduce_scatter | solution.py:633
  526.0 916.4 %reduce-scatter.16.cloned.1.call-start = ((), (), s32[]{:S(2)}) async-start(), calls=%async_computation.13 | async-start | bytes 1769472 | tf_op jit(solution)/shard_map/reduce_scatter | solution.py:606
  685.8 21.8 %collective-permute-start.3 = (bf16[2,384,8,64]{1,3,2,0:T(8,128)(2,1)}, bf16[2,384,8,64]{1,3,2,0:T(8,128)(2,1)}, u32[]{:S(2)}, u32[]{:S(2)}) collective-permute-start(bf16[2,384,8,64]{1,3,2,0:T(8,128)(2,1)} %convert_element_type.647), channel_id=1, source_target_pairs={{0,1},{1,2},{2,3},{3,0},{4,5},{5,6},{6,7},{7,4},{8,9},{9,10},{10,1... | collective-permute-start | bytes 2359304 | tf_op jit(solution)/shard_map/while/body/eval_jaxpr/ppermute | solution.py:22
  690.2 34.2 %collective-permute-start.2 = (bf16[2,384,8,64]{1,3,2,0:T(8,128)(2,1)}, bf16[2,384,8,64]{1,3,2,0:T(8,128)(2,1)}, u32[]{:S(2)}, u32[]{:S(2)}) collective-permute-start(bf16[2,384,8,64]{1,3,2,0:T(8,128)(2,1)} %convert_element_type.645), channel_id=1, source_target_pairs={{0,1},{1,2},{2,3},{3,0},{4,5},{5,6},{6,7},{7,4},{8,9},{9,10},{10,1... | collective-permute-start | bytes 2359304 | tf_op jit(solution)/shard_map/while/body/eval_jaxpr/ppermute | solution.py:22
  692.2 49.0 %collective-permute-start = (bf16[2,384,512]{1,2,0:T(8,128)(2,1)}, bf16[2,384,512]{1,2,0:T(8,128)(2,1)S(1)}, u32[]{:S(2)}, u32[]{:S(2)}) collective-permute-start(bf16[2,384,512]{1,2,0:T(8,128)(2,1)} %copy.176), channel_id=1, source_target_pairs={{0,1},{1,2},{2,3},{4,5},{5,6},{6,7},{8,9},{9,10},{10,11},{12,13},{... | collective-permute-start | bytes 2359304 | tf_op jit(solution)/shard_map/while/body/eval_jaxpr/ppermute | solution.py:16
  694.8 59.9 %collective-permute-start.1 = (bf16[2,384,512]{1,2,0:T(8,128)(2,1)}, bf16[2,384,512]{1,2,0:T(8,128)(2,1)S(1)}, u32[]{:S(2)}, u32[]{:S(2)}) collective-permute-start(bf16[2,384,512]{1,2,0:T(8,128)(2,1)} %copy.177), channel_id=1, source_target_pairs={{0,1},{1,2},{2,3},{4,5},{5,6},{6,7},{8,9},{9,10},{10,11},{12,13},{... | collective-permute-start | bytes 2359304 | tf_op jit(solution)/shard_map/while/body/eval_jaxpr/ppermute | solution.py:16
  759.2 143.5 %copy-start.6 = (f32[2,384,8,64]{1,3,2,0:T(8,128)S(1)}, f32[2,384,8,64]{1,3,2,0:T(8,128)}, u32[]{:S(2)}) copy-start(f32[2,384,8,64]{1,3,2,0:T(8,128)} %get-tuple-element.1522) | copy-start | bytes 4718596 | tf_op jit(solution)/shard_map/while
  760.3 161.3 %collective-permute-start.3 = (bf16[2,384,8,64]{1,3,2,0:T(8,128)(2,1)}, bf16[2,384,8,64]{1,3,2,0:T(8,128)(2,1)}, u32[]{:S(2)}, u32[]{:S(2)}) collective-permute-start(bf16[2,384,8,64]{1,3,2,0:T(8,128)(2,1)} %convert_element_type.647), channel_id=1, source_target_pairs={{0,1},{1,2},{2,3},{3,0},{4,5},{5,6},{6,7},{7,4},{8,9},{9,10},{10,1... | collective-permute-start | bytes 2359304 | tf_op jit(solution)/shard_map/while/body/eval_jaxpr/ppermute | solution.py:22
  903.8 34.2 %collective-permute-start.2 = (bf16[2,384,8,64]{1,3,2,0:T(8,128)(2,1)}, bf16[2,384,8,64]{1,3,2,0:T(8,128)(2,1)}, u32[]{:S(2)}, u32[]{:S(2)}) collective-permute-start(bf16[2,384,8,64]{1,3,2,0:T(8,128)(2,1)} %convert_element_type.645), channel_id=1, source_target_pairs={{0,1},{1,2},{2,3},{3,0},{4,5},{5,6},{6,7},{7,4},{8,9},{9,10},{10,1... | collective-permute-start | bytes 2359304 | tf_op jit(solution)/shard_map/while/body/eval_jaxpr/ppermute | solution.py:22
  906.4 48.3 %collective-permute-start = (bf16[2,384,512]{1,2,0:T(8,128)(2,1)}, bf16[2,384,512]{1,2,0:T(8,128)(2,1)S(1)}, u32[]{:S(2)}, u32[]{:S(2)}) collective-permute-start(bf16[2,384,512]{1,2,0:T(8,128)(2,1)} %copy.176), channel_id=1, source_target_pairs={{0,1},{1,2},{2,3},{4,5},{5,6},{6,7},{8,9},{9,10},{10,11},{12,13},{... | collective-permute-start | bytes 2359304 | tf_op jit(solution)/shard_map/while/body/eval_jaxpr/ppermute | solution.py:16
  909.0 58.3 %collective-permute-start.1 = (bf16[2,384,512]{1,2,0:T(8,128)(2,1)}, bf16[2,384,512]{1,2,0:T(8,128)(2,1)S(1)}, u32[]{:S(2)}, u32[]{:S(2)}) collective-permute-start(bf16[2,384,512]{1,2,0:T(8,128)(2,1)} %copy.177), channel_id=1, source_target_pairs={{0,1},{1,2},{2,3},{4,5},{5,6},{6,7},{8,9},{9,10},{10,11},{12,13},{... | collective-permute-start | bytes 2359304 | tf_op jit(solution)/shard_map/while/body/eval_jaxpr/ppermute | solution.py:16
  972.9 162.0 %collective-permute-start.3 = (bf16[2,384,8,64]{1,3,2,0:T(8,128)(2,1)}, bf16[2,384,8,64]{1,3,2,0:T(8,128)(2,1)}, u32[]{:S(2)}, u32[]{:S(2)}) collective-permute-start(bf16[2,384,8,64]{1,3,2,0:T(8,128)(2,1)} %convert_element_type.647), channel_id=1, source_target_pairs={{0,1},{1,2},{2,3},{3,0},{4,5},{5,6},{6,7},{7,4},{8,9},{9,10},{10,1... | collective-permute-start | bytes 2359304 | tf_op jit(solution)/shard_map/while/body/eval_jaxpr/ppermute | solution.py:22
  976.3 170.5 %collective-permute-start.2 = (bf16[2,384,8,64]{1,3,2,0:T(8,128)(2,1)}, bf16[2,384,8,64]{1,3,2,0:T(8,128)(2,1)}, u32[]{:S(2)}, u32[]{:S(2)}) collective-permute-start(bf16[2,384,8,64]{1,3,2,0:T(8,128)(2,1)} %convert_element_type.645), channel_id=1, source_target_pairs={{0,1},{1,2},{2,3},{3,0},{4,5},{5,6},{6,7},{7,4},{8,9},{9,10},{10,1... | collective-permute-start | bytes 2359304 | tf_op jit(solution)/shard_map/while/body/eval_jaxpr/ppermute | solution.py:22
  1119.7 35.2 %collective-permute-start = (bf16[2,384,512]{1,2,0:T(8,128)(2,1)}, bf16[2,384,512]{1,2,0:T(8,128)(2,1)S(1)}, u32[]{:S(2)}, u32[]{:S(2)}) collective-permute-start(bf16[2,384,512]{1,2,0:T(8,128)(2,1)} %copy.176), channel_id=1, source_target_pairs={{0,1},{1,2},{2,3},{4,5},{5,6},{6,7},{8,9},{9,10},{10,11},{12,13},{... | collective-permute-start | bytes 2359304 | tf_op jit(solution)/shard_map/while/body/eval_jaxpr/ppermute | solution.py:16
  1122.3 43.7 %collective-permute-start.1 = (bf16[2,384,512]{1,2,0:T(8,128)(2,1)}, bf16[2,384,512]{1,2,0:T(8,128)(2,1)S(1)}, u32[]{:S(2)}, u32[]{:S(2)}) collective-permute-start(bf16[2,384,512]{1,2,0:T(8,128)(2,1)} %copy.177), channel_id=1, source_target_pairs={{0,1},{1,2},{2,3},{4,5},{5,6},{6,7},{8,9},{9,10},{10,11},{12,13},{... | collective-permute-start | bytes 2359304 | tf_op jit(solution)/shard_map/while/body/eval_jaxpr/ppermute | solution.py:16
  1170.5 17.2 copy-start.6
  1171.5 175.6 %collective-permute-start.3 = (bf16[2,384,8,64]{1,3,2,0:T(8,128)(2,1)}, bf16[2,384,8,64]{1,3,2,0:T(8,128)(2,1)}, u32[]{:S(2)}, u32[]{:S(2)}) collective-permute-start(bf16[2,384,8,64]{1,3,2,0:T(8,128)(2,1)} %convert_element_type.647), channel_id=1, source_target_pairs={{0,1},{1,2},{2,3},{3,0},{4,5},{5,6},{6,7},{7,4},{8,9},{9,10},{10,1... | collective-permute-start | bytes 2359304 | tf_op jit(solution)/shard_map/while/body/eval_jaxpr/ppermute | solution.py:22
  1188.7 169.6 %collective-permute-start.2 = (bf16[2,384,8,64]{1,3,2,0:T(8,128)(2,1)}, bf16[2,384,8,64]{1,3,2,0:T(8,128)(2,1)}, u32[]{:S(2)}, u32[]{:S(2)}) collective-permute-start(bf16[2,384,8,64]{1,3,2,0:T(8,128)(2,1)} %convert_element_type.645), channel_id=1, source_target_pairs={{0,1},{1,2},{2,3},{3,0},{4,5},{5,6},{6,7},{7,4},{8,9},{9,10},{10,1... | collective-permute-start | bytes 2359304 | tf_op jit(solution)/shard_map/while/body/eval_jaxpr/ppermute | solution.py:22
  1192.0 168.7 %collective-permute-start = (bf16[2,384,512]{1,2,0:T(8,128)(2,1)}, bf16[2,384,512]{1,2,0:T(8,128)(2,1)S(1)}, u32[]{:S(2)}, u32[]{:S(2)}) collective-permute-start(bf16[2,384,512]{1,2,0:T(8,128)(2,1)} %copy.176), channel_id=1, source_target_pairs={{0,1},{1,2},{2,3},{4,5},{5,6},{6,7},{8,9},{9,10},{10,11},{12,13},{... | collective-permute-start | bytes 2359304 | tf_op jit(solution)/shard_map/while/body/eval_jaxpr/ppermute | solution.py:16
  1333.4 28.5 %collective-permute-start.1 = (bf16[2,384,512]{1,2,0:T(8,128)(2,1)}, bf16[2,384,512]{1,2,0:T(8,128)(2,1)S(1)}, u32[]{:S(2)}, u32[]{:S(2)}) collective-permute-start(bf16[2,384,512]{1,2,0:T(8,128)(2,1)} %copy.177), channel_id=1, source_target_pairs={{0,1},{1,2},{2,3},{4,5},{5,6},{6,7},{8,9},{9,10},{10,11},{12,13},{... | collective-permute-start | bytes 2359304 | tf_op jit(solution)/shard_map/while/body/eval_jaxpr/ppermute | solution.py:16
  1380.5 97.7 %reduce-scatter.26.cloned.1.call-start = ((), (), s32[]{:S(2)}) async-start(), calls=%async_computation.18 | async-start | bytes 2359296 | tf_op jit(solution)/shard_map/reduce_scatter | solution.py:645
  1386.3 128.7 %reduce-scatter.24.cloned.1.call-start = ((), (), s32[]{:S(2)}) async-start(), calls=%async_computation.17 | async-start | bytes 2359296 | tf_op jit(solution)/shard_map/reduce_scatter | solution.py:642
  1392.2 159.7 %reduce-scatter.20.cloned.1.call-start = ((), (), s32[]{:S(2)}) async-start(), calls=%async_computation.15 | async-start | bytes 2359296 | tf_op jit(solution)/shard_map/reduce_scatter | solution.py:621
  1398.5 190.3 %reduce-scatter.14.cloned.1.call-start = ((), (), s32[]{:S(2)}) async-start(), calls=%async_computation.12 | async-start | bytes 2359296 | tf_op jit(solution)/shard_map/reduce_scatter | solution.py:597
  1409.6 215.7 %reduce-scatter.12.cloned.1.call-start = ((), (), s32[]{:S(2)}) async-start(), calls=%async_computation.11 | async-start | bytes 2359296 | tf_op jit(solution)/shard_map/reduce_scatter | solution.py:594
  1409.6 8.6 copy-start.41
  1418.4 7.5 copy-start.34
  1421.7 203.6 %copy-start.21 = (bf16[2,384,512]{2,1,0:T(8,128)(2,1)S(1)}, bf16[2,384,512]{2,1,0:T(8,128)(2,1)}, u32[]{:S(2)}) copy-start(bf16[2,384,512]{2,1,0:T(8,128)(2,1)} %param.35) | copy-start | bytes 2359300
  1421.7 203.6 %copy-start.63 = (f32[768]{0:T(1024)S(1)}, f32[768]{0:T(1024)}, u32[]{:S(2)}) copy-start(f32[768]{0:T(1024)} %copy-done.62) | copy-start | bytes 9220
  1421.7 203.6 %copy-start.79 = (f32[512]{0:T(512)S(1)}, f32[512]{0:T(512)}, u32[]{:S(2)}) copy-start(f32[512]{0:T(512)} %copy-done.78) | copy-start | bytes 6148
  1421.7 241.7 %reduce-scatter.28.cloned.1.call-start = ((), (), s32[]{:S(2)}) async-start(), calls=%async_computation.19 | async-start | bytes 294912
  1423.1 301.0 %all-reduce.38.cloned.1.call-start = ((), (), s32[]{:S(2)}) async-start(), calls=%async_computation.20 | async-start | bytes 3407872 | tf_op jit(solution)/shard_map/psum | solution.py:658
  1659.9 76.1 %copy-start.1 = (bf16[512,2048]{1,0:T(8,128)(2,1)S(1)}, bf16[512,2048]{1,0:T(8,128)(2,1)}, u32[]{:S(2)}) copy-start(bf16[512,2048]{1,0:T(8,128)(2,1)} %param.56) | copy-start | bytes 6291460
  1724.1 10.3 copy-start.47
  1724.1 11.1 copy-start.46
  (103 other events, 350.1 us)
Sparse Core Ops, SparseCore 0:
  28.2 46.6 all-gather.4
  76.8 43.9 all-gather.2
  519.0 111.2 reduce-scatter.17
  632.5 30.4 reduce-scatter.21
  1380.6 61.7 reduce-scatter.15
  1444.6 33.5 reduce-scatter.25
  1480.7 34.2 reduce-scatter.23
  1517.4 34.4 reduce-scatter.19
  1554.3 34.4 reduce-scatter.13
  1591.0 34.1 reduce-scatter.11
  1628.2 29.0 reduce-scatter.27
  1661.1 62.9 all-reduce.37
where the time goes:
time: 1740 us
  waiting for transfers between devices  568 us (33%)
  starting transfers between devices  562 us (32%)
  local copies, waits for them, and re-layouts  247 us (14%)
  other arithmetic  182 us (10%)
  matrix products  106 us (6%)
  blocking collectives  43.2 us (2%)
  between operations  18.6 us (1%)
    ppermute x8, starting transfers between devices, from_behind(): return lax.ppermute(value, axis, pairs)  316 us
    ppermute x10, starting transfers between devices, passed_along(): return lax.ppermute(block, axis, route)  245 us
    ppermute x10, waiting for transfers between devices, passed_along(): return lax.ppermute(block, axis, route)  161 us
    ppermute x8, waiting for transfers between devices, from_behind(): return lax.ppermute(value, axis, pairs)  89.5 us
    cond x26, local copies, waits for them, and re-layouts  58.8 us
    all_gather x1, waiting for transfers between devices, attend_forward(): lax.all_gather(key_rows, 'tm', axis=1, tiled=True)  41.2 us
    all_gather x1, waiting for transfers between devices, attend_forward(): lax.all_gather(value_rows, 'tm', axis=1, tiled=True)  39.8 us
    reduce_scatter x1, waiting for transfers between devices, body(): lax.psum_scatter(gradient_list[11].astype(jnp.bfloat16), 'rows', scatter_...  36.9 us
  transfers between devices with their start and end apart: 30, of which 26 were waited for; matrix products, arithmetic and copies ran while one was open for 16% of the time, Pallas kernels for 0%

commit v1 on v0

v1 whole, which is shorter than its diff:
```python
import functools

import jax
import jax.numpy as jnp
from jax import lax
from jax.experimental import pallas as pl
from jax.experimental.pallas import tpu as pltpu
from jax.sharding import PartitionSpec as P

EPSILON = 1e-05
NEGATIVE = -1e30
HIGHEST = lax.Precision.HIGHEST
BFLOAT = jnp.bfloat16
FLOAT = jnp.float32
NEG = NEGATIVE
F32 = FLOAT
BF = BFLOAT


def passed_along(block, axis, distance):
    devices = range(lax.axis_size(axis))
    route = [(i - distance, i) for i in devices if i - distance in devices]
    return lax.ppermute(block, axis, route)


def boundaries(seq_total):
    edges_list = list(range(1, 16))
    for exponent in range(16):
        edges_list.append(int(16.0 * (seq_total / 16.0) ** (exponent / 16.0)))
    return edges_list


def nt(a,b): return lax.dot_general(a,b,(((1,),(1,)),((),())),preferred_element_type=F32)
def nn(a,b): return lax.dot_general(a,b,(((1,),(0,)),((),())),preferred_element_type=F32)

def strip_kernel(base_ref, out_ref):
    nh,T,L=out_ref.shape
    for h in range(nh):
        e=base_ref[h]
        for g in range(T//8):
            out_ref[h,8*g:8*g+8,:]=pltpu.roll(e,8*g,1)[:,T:] if g else e[:,T:]

def make_strip(base8,T,L):
    nh=base8.shape[0]
    return pl.pallas_call(strip_kernel,out_shape=jax.ShapeDtypeStruct((nh,T,L),F32),
        compiler_params=pltpu.CompilerParams(vmem_limit_bytes=40*2**20))(base8)

def headmask(shape,h):
    lane=lax.broadcasted_iota(jnp.int32,shape,1)
    return (lane>=64*h)&(lane<64*h+64), lane==((64*h+64)%128)

def fwd_kernel(len_ref,x_ref,b_ref,o_ref,ot_ref,lse_ref,kh,vt,acc,*,nh,BQ):
    G=x_ref.shape[0]; T=x_ref.shape[3]
    n=len_ref[pl.program_id(0)]
    nk=(n+T-1)//T
    def prep(t,_):
        k=x_ref[t,1,0].astype(F32)
        pos=t*T+lax.broadcasted_iota(jnp.int32,(T,128),0)
        for h in range(nh):
            hm,sp=headmask((T,128),h)
            kh[h,t]=jnp.where(hm,k,jnp.where(sp&(pos>=n),NEG,0.0)).astype(BF)
        vt[t]=x_ref[t,2,0].T
        return 0
    lax.fori_loop(0,nk,prep,0)
    def qloop(qb,_):
        q=x_ref[qb,0,0].astype(F32)*0.125
        for h in range(nh):
            acc[h]=jnp.zeros((64,T),F32)
        qh=[]
        for h in range(nh):
            hm,sp=headmask((T,128),h)
            qh.append(jnp.where(hm,q,jnp.where(sp,1.0,0.0)).astype(BF))
        def kloop(kb,c):
            off=pl.multiple_of((qb-kb)*T,128)
            res=[]
            for h in range(nh):
                m,l=c[h]
                s=nt(kh[h,kb],qh[h])+b_ref[h,:,pl.ds(off,T)]
                mn=jnp.maximum(m,jnp.max(s,axis=0,keepdims=True))
                p=jnp.exp(s-mn)
                al=jnp.exp(m-mn)
                l=l*al+jnp.sum(p,axis=0,keepdims=True)
                acc[h]=acc[h]*al+nn(vt[kb,64*h:64*h+64,:],p.astype(BF))
                res.append((mn,l))
            return tuple(res)
        c=lax.fori_loop(0,jnp.minimum(qb+1,nk),kloop,tuple((jnp.full((1,T),NEG,F32),jnp.zeros((1,T),F32)) for _ in range(nh)))
        for h in range(nh):
            m,l=c[h]
            lse_ref[0,h,qb]=m+jnp.log(l)
            ot_ref[0,qb,64*h:64*h+64,:]=acc[h]/l
        if nh==1: ot_ref[0,qb,64:128,:]=jnp.zeros((64,T),F32)
        o_ref[qb,0]=ot_ref[0,qb].T.astype(BF)
        return 0
    lax.fori_loop(0,G,qloop,0)

def attn_fwd(lengths,x,strip,nh):
    G,_,R,T,W=x.shape; L=G*T
    gs=pltpu.PrefetchScalarGridSpec(num_scalar_prefetch=1,grid=(R,),
      in_specs=[pl.BlockSpec((G,3,1,T,W),lambda r,l:(0,0,r,0,0)),pl.BlockSpec((nh,T,L),lambda r,l:(0,0,0))],
      out_specs=[pl.BlockSpec((G,1,T,W),lambda r,l:(0,r,0,0)),pl.BlockSpec((1,G,W,T),lambda r,l:(r,0,0,0)),pl.BlockSpec((1,nh,G,1,T),lambda r,l:(r,0,0,0,0))],
      scratch_shapes=[pltpu.VMEM((nh,G,T,W),BF),pltpu.VMEM((G,W,T),BF),pltpu.VMEM((nh,64,T),F32)])
    return pl.pallas_call(functools.partial(fwd_kernel,nh=nh,BQ=T),grid_spec=gs,
      out_shape=[jax.ShapeDtypeStruct((G,R,T,W),BF),jax.ShapeDtypeStruct((R,G,W,T),F32),jax.ShapeDtypeStruct((R,nh,G,1,T),F32)],
      compiler_params=pltpu.CompilerParams(vmem_limit_bytes=56*2**20))(lengths,x,strip)

def bwd_kernel(len_ref,x_ref,do_ref,ot_ref,lse_ref,b_ref,dx_ref,db_ref,kh,vh,qh,qs,kt,dqt,dl,dk,dv,dbs,*,nh):
    G=x_ref.shape[0]; T=x_ref.shape[3]; L=G*T
    r=pl.program_id(0)
    n=len_ref[r]
    nk=(n+T-1)//T
    @pl.when(r==0)
    def _(): dbs[...]=jnp.zeros_like(dbs)
    def prepq(t,_):
        q=x_ref[t,0,0].astype(F32)*0.125
        qs[t]=q.astype(BF)
        for h in range(nh):
            hm,sp=headmask((T,128),h)
            qh[h,t]=jnp.where(hm,q,jnp.where(sp,1.0,0.0)).astype(BF)
        pr=do_ref[t,0].astype(F32).T*ot_ref[0,t]
        for h in range(nh):
            dl[h,t]=jnp.sum(pr[64*h:64*h+64],axis=0,keepdims=True)
        dqt[t]=jnp.zeros((128,T),F32)
        return 0
    lax.fori_loop(0,G,prepq,0)
    def kloop(kb,_):
        k=x_ref[kb,1,0].astype(F32)
        v=x_ref[kb,2,0].astype(F32)
        kt[...]=x_ref[kb,1,0].T
        pos=kb*T+lax.broadcasted_iota(jnp.int32,(T,128),0)
        for h in range(nh):
            hm,sp=headmask((T,128),h)
            kh[h]=jnp.where(hm,k,jnp.where(sp&(pos>=n),NEG,0.0)).astype(BF)
            vh[h]=jnp.where(hm,v,0.0).astype(BF)
        dk[...]=jnp.zeros_like(dk); dv[...]=jnp.zeros_like(dv)
        def qloop(qb,_):
            off=pl.multiple_of((qb-kb)*T,128)
            do=do_ref[qb,0]; q=qs[qb]
            for h in range(nh):
                s=nt(kh[h],qh[h,qb])+b_ref[h,:,pl.ds(off,T)]
                p=jnp.exp(s-lse_ref[0,h,qb])
                dp=nt(vh[h],do)
                ds=p*(dp-dl[h,qb])
                dsb=ds.astype(BF)
                dv[h]+=nn(p.astype(BF),do)
                dk[h]+=nn(dsb,q)
                dqt[qb,64*h:64*h+64,:]+=nn(kt[64*h:64*h+64,:],dsb)
                dbs[h,:,pl.ds(off,T)]+=ds
            return 0
        lax.fori_loop(kb,G,qloop,0)
        if nh==2:
            hm,_=headmask((T,128),0)
            dx_ref[kb,1,0]=jnp.where(hm,dk[0],dk[1]).astype(BF)
            dx_ref[kb,2,0]=jnp.where(hm,dv[0],dv[1]).astype(BF)
        else:
            dx_ref[kb,1,0]=dk[0].astype(BF)
            dx_ref[kb,2,0]=dv[0].astype(BF)
        return 0
    lax.fori_loop(0,nk,kloop,0)
    def zloop(kb,_):
        dx_ref[kb,1,0]=jnp.zeros((T,128),BF)
        dx_ref[kb,2,0]=jnp.zeros((T,128),BF)
        return 0
    lax.fori_loop(nk,G,zloop,0)
    def oloop(t,_):
        dx_ref[t,0,0]=(dqt[t]*0.125).T.astype(BF)
        return 0
    lax.fori_loop(0,G,oloop,0)
    @pl.when(r==pl.num_programs(0)-1)
    def _():
        for h in range(nh):
            a=dbs[h,0:8,:]
            for g in range(1,T//8):
                a=a+pltpu.roll(dbs[h,8*g:8*g+8,:],L-8*g,1)
            db_ref[h]=a

def attn_bwd(lengths,x,do,ot,lse,strip,nh):
    G,_,R,T,W=x.shape; L=G*T
    gs=pltpu.PrefetchScalarGridSpec(num_scalar_prefetch=1,grid=(R,),
      in_specs=[pl.BlockSpec((G,3,1,T,W),lambda r,l:(0,0,r,0,0)),pl.BlockSpec((G,1,T,W),lambda r,l:(0,r,0,0)),
        pl.BlockSpec((1,G,W,T),lambda r,l:(r,0,0,0)),pl.BlockSpec((1,nh,G,1,T),lambda r,l:(r,0,0,0,0)),pl.BlockSpec((nh,T,L),lambda r,l:(0,0,0))],
      out_specs=[pl.BlockSpec((G,3,1,T,W),lambda r,l:(0,0,r,0,0)),pl.BlockSpec((nh,8,L),lambda r,l:(0,0,0))],
      scratch_shapes=[pltpu.VMEM((nh,T,W),BF),pltpu.VMEM((nh,T,W),BF),pltpu.VMEM((nh,G,T,W),BF),pltpu.VMEM((G,T,W),BF),pltpu.VMEM((W,T),BF),
        pltpu.VMEM((G,W,T),F32),pltpu.VMEM((nh,G,1,T),F32),pltpu.VMEM((nh,T,W),F32),pltpu.VMEM((nh,T,W),F32),pltpu.VMEM((nh,T,L),F32)])
    return pl.pallas_call(functools.partial(bwd_kernel,nh=nh),grid_spec=gs,
      out_shape=[jax.ShapeDtypeStruct((G,3,R,T,W),BF),jax.ShapeDtypeStruct((nh,8,L),F32)],
      compiler_params=pltpu.CompilerParams(vmem_limit_bytes=58*2**20))(lengths,x,do,ot,lse,strip)


def tn(a, b):
    return lax.dot_general(a, b, (((0,), (0,)), ((), ())), preferred_element_type=F32)


def sigmoid(v):
    return 0.5 * jnp.tanh(0.5 * v) + 0.5


def row(ref):
    return ref[...].astype(F32)


def norm_parts(v):
    center = v - jnp.mean(v, axis=-1, keepdims=True)
    inverse = lax.rsqrt(jnp.mean(center * center, axis=-1, keepdims=True) + EPSILON)
    return center * inverse, inverse


def norm_pull(n, inverse, gain, grad):
    dn = grad * gain
    return (
        dn - jnp.mean(dn, axis=-1, keepdims=True) - n * jnp.mean(dn * n, axis=-1, keepdims=True)
    ) * inverse


def add_rows(ref, place, values):
    total = jnp.sum(values, axis=0, keepdims=True)
    for c in range(values.shape[1] // 512):
        ref[place + c : place + c + 1, :] += total[:, 512 * c : 512 * c + 512]


def start_small(ref):
    @pl.when(pl.program_id(0) == 0)
    def _():
        ref[...] = jnp.zeros_like(ref)


def put_heads(write, value, nh):
    for pair in range(value.shape[1] // 128):
        part = value[:, 128 * pair : 128 * pair + 128]
        if nh == 2:
            write(pair, part.astype(BF))
        else:
            low = lax.broadcasted_iota(jnp.int32, part.shape, 1) < 64
            write(2 * pair, jnp.where(low, part, 0.0).astype(BF))
            write(2 * pair + 1, jnp.where(low, pltpu.roll(part, 64, 1), 0.0).astype(BF))


def take_heads(read, units, nh):
    if nh == 2:
        return jnp.concatenate([read(u) for u in range(units)], axis=1)
    pairs = [
        (read(2 * u).astype(F32) + pltpu.roll(read(2 * u + 1).astype(F32), 64, 1)).astype(BF)
        for u in range(units // 2)
    ]
    return jnp.concatenate(pairs, axis=1)


def open_kernel(
    x_ref, g1, s1, wu, wd, g2, s2, wi, x1_ref, h1_ref, a_ref, sp_ref, h2_ref, u_ref, *, nh
):
    x0 = x_ref[0].astype(F32)
    n, _ = norm_parts(x0)
    h1 = (n * row(g1) + row(s1)).astype(BF)
    h1_ref[0] = h1
    y = None
    for f in range(wu.shape[1] // 512):
        at = slice(512 * f, 512 * f + 512)
        z = nn(h1, wu[:, at])
        sig = sigmoid(z)
        a = (z * sig).astype(BF)
        a_ref[0, :, at] = a
        sp_ref[0, :, at] = (sig * (1.0 + z * (1.0 - sig))).astype(BF)
        part = nn(a, wd[at, :])
        y = part if y is None else y + part
    x1 = x0 + 0.5 * y
    x1_ref[0] = x1
    n, _ = norm_parts(x1)
    h2 = (n * row(g2) + row(s2)).astype(BF)
    h2_ref[0] = h2
    for kind in range(3):

        def write(unit, part):
            u_ref[unit, 0, kind, 0] = part

        put_heads(write, nn(h2, wi[:, 512 * kind : 512 * kind + 512]), nh)


def gate_kernel(
    len_ref, o_ref, x1_ref, wo, g3, s3, wc, att_ref, x2_ref, h3_ref, g_ref, ga_ref, gb_ref, *, nh
):
    units = o_ref.shape[0]
    rows = x1_ref.shape[1]
    att = take_heads(lambda u: o_ref[u, 0, 0], units, nh)
    att_ref[0] = att
    x2 = x1_ref[0] + nn(att, wo[...])
    x2_ref[0] = x2
    n, _ = norm_parts(x2)
    h3 = (n * row(g3) + row(s3)).astype(BF)
    h3_ref[0] = h3
    channels = g_ref.shape[2]
    limit = len_ref[pl.program_id(0)] - len_ref[len_ref.shape[0] - 1]
    place = lax.broadcasted_iota(jnp.int32, (rows, 1), 0)
    valid = jnp.where(place < limit, 1.0, 0.0)
    for f in range(channels // 512):
        at = slice(512 * f, 512 * f + 512)
        lin = nn(h3, wc[:, at])
        gate = nn(h3, wc[:, channels + 512 * f : channels + 512 * f + 512])
        sig = sigmoid(gate)
        sv = sig * valid
        g = lin * sv
        g_ref[0, :, at] = g.astype(BF)
        ga_ref[0, :, at] = sv.astype(BF)
        gb_ref[0, :, at] = (g * (1.0 - sig)).astype(BF)


def middle_kernel(
    g_ref, halo_ref, x2_ref, cot_ref, dep, ig, si, wco, lg, ls, wu, wd, fg, fs,
    out_ref, dx3_ref, dg_ref, dhalo_ref, small_ref, ddep_ref, pack_ref,
    gx, cs, dcx, sp3, h4s, a4s, sp4, dz4s, dy4s, a3s, dy3s,
):
    rec = pl.program_id(0)
    rows = x2_ref.shape[1]
    channels = g_ref.shape[2]
    taps = dep.shape[0] - 1
    start_small(small_ref)
    start_small(ddep_ref)
    mine = pl.ds(pl.multiple_of(rec * rows, 128), rows)
    gx[0:16, :] = halo_ref[0].astype(F32)
    gx[16:, :] = g_ref[0].astype(F32)
    for c in range(channels // 128):
        at = slice(128 * c, 128 * c + 128)
        total = dep[0:1, at] * gx[2 : 2 + rows, at]
        for r in range(1, taps):
            total = total + dep[r : r + 1, at] * gx[2 + r : 2 + r + rows, at]
        cs[:, at] = total
    n3, inv3 = norm_parts(cs[...])
    cs[...] = n3
    w = n3 * row(ig) + row(si)
    sig = sigmoid(w)
    a3 = (w * sig).astype(BF)
    a3s[mine, :] = a3
    sp3[...] = (sig * (1.0 + w * (1.0 - sig))).astype(BF)
    x3 = x2_ref[0] + nn(a3, wco[...])
    n4, inv4 = norm_parts(x3)
    h4 = (n4 * row(lg) + row(ls)).astype(BF)
    h4s[mine, :] = h4
    y = None
    for f in range(wu.shape[1] // 512):
        at = slice(512 * f, 512 * f + 512)
        z = nn(h4, wu[:, at])
        sig = sigmoid(z)
        a = (z * sig).astype(BF)
        a4s[mine, at] = a
        sp4[:, at] = (sig * (1.0 + z * (1.0 - sig))).astype(BF)
        part = nn(a, wd[at, :])
        y = part if y is None else y + part
    x4 = x3 + 0.5 * y
    n5, inv5 = norm_parts(x4)
    out_ref[0] = (n5 * row(fg) + row(fs)).astype(BF)
    cot = cot_ref[0].astype(F32)
    add_rows(small_ref, 8, cot * n5)
    add_rows(small_ref, 9, cot)
    dx4 = norm_pull(n5, inv5, row(fg), cot)
    dy4 = (0.5 * dx4).astype(BF)
    dy4s[mine, :] = dy4
    dh = None
    for f in range(wu.shape[1] // 512):
        at = slice(512 * f, 512 * f + 512)
        dz = (nt(dy4, wd[at, :]) * sp4[:, at].astype(F32)).astype(BF)
        dz4s[mine, at] = dz
        part = nt(dz, wu[:, at])
        dh = part if dh is None else dh + part
    add_rows(small_ref, 6, dh * n4)
    add_rows(small_ref, 7, dh)
    dx3 = dx4 + norm_pull(n4, inv4, row(lg), dh)
    dx3_ref[0] = dx3
    dy3 = dx3.astype(BF)
    dy3s[mine, :] = dy3
    dw = nt(dy3, wco[...]) * sp3[...].astype(F32)
    n3 = cs[...]
    add_rows(small_ref, 2, dw * n3)
    add_rows(small_ref, 4, dw)
    dcx[0:16, :] = jnp.zeros((16, channels), F32)
    dcx[16 + rows :, :] = jnp.zeros((16, channels), F32)
    dcx[16 : 16 + rows, :] = norm_pull(n3, inv3, row(ig), dw)
    for c in range(channels // 128):
        at = slice(128 * c, 128 * c + 128)
        dc = dcx[16 : 16 + rows, at]
        for r in range(taps):
            ddep_ref[r : r + 1, at] += jnp.sum(
                dc * gx[2 + r : 2 + r + rows, at], axis=0, keepdims=True
            )
        total = dep[0:1, at] * dcx[14 : 30 + rows, at]
        for r in range(1, taps):
            total = total + dep[r : r + 1, at] * dcx[14 - r : 30 - r + rows, at]
        dhalo_ref[0, :, at] = total[0:16].astype(BF)
        dg_ref[0, :, at] = total[16:].astype(BF)

    @pl.when(rec == pl.num_programs(0) - 1)
    def _():
        count = pack_ref.shape[0]
        place = 0
        for f in range(wu.shape[1] // 512):
            at = slice(512 * f, 512 * f + 512)
            put_share(pack_ref, place, tn(h4s[...], dz4s[:, at]), 0, 1)
            place += 512 // count
        for f in range(wd.shape[0] // 512):
            at = slice(512 * f, 512 * f + 512)
            put_share(pack_ref, place, tn(a4s[:, at], dy4s[...]), f, wd.shape[0] // 512)
        place += wd.shape[0] // count
        for f in range(channels // 512):
            at = slice(512 * f, 512 * f + 512)
            put_share(pack_ref, place, tn(a3s[:, at], dy3s[...]), f, channels // 512)


def put_share(pack_ref, place, block, index, blocks):
    count = pack_ref.shape[0]
    height = 512 * blocks // count
    if height >= 512:
        shard, within = divmod(512 * index, height)
        pack_ref[shard, place + within : place + within + 512, :] = block.astype(BF)
        return
    held = 512 // height
    pack_ref[held * index : held * index + held, place : place + height, :] = block.reshape(
        held, height, 512
    ).astype(BF)


def ungate_kernel(
    dg_ref, back_ref, ga_ref, gb_ref, dx3_ref, x2_ref, g3, wc, wo,
    dx2_ref, du_ref, dy2_ref, do_ref, small_ref, dgx, *, nh,
):
    start_small(small_ref)
    rows = x2_ref.shape[1]
    channels = ga_ref.shape[2]
    dgx[...] = dg_ref[0].astype(F32)
    dgx[rows - 16 :, :] += back_ref[0].astype(F32)
    dh = None
    for f in range(channels // 512):
        at = slice(512 * f, 512 * f + 512)
        up = slice(channels + 512 * f, channels + 512 * f + 512)
        dg = dgx[:, at]
        lin = (dg * ga_ref[0, :, at].astype(F32)).astype(BF)
        gate = (dg * gb_ref[0, :, at].astype(F32)).astype(BF)
        du_ref[0, :, at] = lin
        du_ref[0, :, up] = gate
        part = nt(lin, wc[:, at]) + nt(gate, wc[:, up])
        dh = part if dh is None else dh + part
    n, inverse = norm_parts(x2_ref[0])
    add_rows(small_ref, 0, dh * n)
    add_rows(small_ref, 1, dh)
    dx2 = dx3_ref[0] + norm_pull(n, inverse, row(g3), dh)
    dx2_ref[0] = dx2
    dy2 = dx2.astype(BF)
    dy2_ref[0] = dy2

    def write(unit, part):
        do_ref[unit, 0, 0] = part

    put_heads(write, nt(dy2, wo[...]), nh)


def close_kernel(
    u_ref, h2_ref, x1_ref, dx2_ref, x_ref, h1_ref, a_ref, sp_ref, g1, wu, wd, g2, wi,
    out_ref, small_ref, pack_ref, dps, h2s, h1s, a1s, dzs, dys, *, nh,
):
    rec = pl.program_id(0)
    rows = x1_ref.shape[1]
    start_small(small_ref)
    mine = pl.ds(pl.multiple_of(rec * rows, 128), rows)
    h2s[mine, :] = h2_ref[0]
    h1s[mine, :] = h1_ref[0]
    a1s[mine, :] = a_ref[0]
    dh = None
    for kind in range(3):
        at = slice(512 * kind, 512 * kind + 512)
        dp = take_heads(lambda u: u_ref[u, 0, kind, 0], u_ref.shape[0], nh)
        dps[mine, at] = dp
        part = nt(dp, wi[:, at])
        dh = part if dh is None else dh + part
    n, inverse = norm_parts(x1_ref[0])
    add_rows(small_ref, 2, dh * n)
    add_rows(small_ref, 3, dh)
    dx1 = dx2_ref[0] + norm_pull(n, inverse, row(g2), dh)
    dy = (0.5 * dx1).astype(BF)
    dys[mine, :] = dy
    dh = None
    for f in range(wu.shape[1] // 512):
        at = slice(512 * f, 512 * f + 512)
        dz = (nt(dy, wd[at, :]) * sp_ref[0, :, at].astype(F32)).astype(BF)
        dzs[mine, at] = dz
        part = nt(dz, wu[:, at])
        dh = part if dh is None else dh + part
    n, inverse = norm_parts(x_ref[0].astype(F32))
    add_rows(small_ref, 0, dh * n)
    add_rows(small_ref, 1, dh)
    out_ref[0] = (dx1 + norm_pull(n, inverse, row(g1), dh)).astype(BF)

    @pl.when(rec == pl.num_programs(0) - 1)
    def _():
        count = pack_ref.shape[0]
        place = 0
        for f in range(wi.shape[1] // 512):
            at = slice(512 * f, 512 * f + 512)
            put_share(pack_ref, place, tn(h2s[...], dps[:, at]), 0, 1)
            place += 512 // count
        for f in range(wu.shape[1] // 512):
            at = slice(512 * f, 512 * f + 512)
            put_share(pack_ref, place, tn(h1s[...], dzs[:, at]), 0, 1)
            place += 512 // count
        for f in range(wd.shape[0] // 512):
            at = slice(512 * f, 512 * f + 512)
            put_share(pack_ref, place, tn(a1s[:, at], dys[...]), f, wd.shape[0] // 512)


def weights_kernel(h3_ref, du_ref, att_ref, dy_ref, pack_ref):
    count = pack_ref.shape[0]
    place = 0
    for f in range(du_ref.shape[1] // 512):
        at = slice(512 * f, 512 * f + 512)
        put_share(pack_ref, place, tn(h3_ref[...], du_ref[:, at]), 0, 1)
        place += 512 // count
    put_share(pack_ref, place, tn(att_ref[...], dy_ref[...]), 0, 1)


def per_rec(array):
    shape = (1,) + array.shape[1:]
    tail = (0,) * (array.ndim - 1)
    return pl.BlockSpec(shape, lambda r, *_: (r,) + tail)


def whole(array):
    zeros = (0,) * array.ndim
    return pl.BlockSpec(array.shape, lambda r, *_: zeros)


def per_unit(array, recs):
    units, rest = array.shape[0], array.shape[2:]
    if array.ndim == 6:
        return pl.BlockSpec(
            (units, 1, rest[0], 1) + rest[2:], lambda r, *_: (0, r // recs, 0, r % recs, 0, 0)
        )
    return pl.BlockSpec((units, 1, 1) + rest[1:], lambda r, *_: (0, r // recs, r % recs, 0, 0))


def spot(shape, kind=F32):
    return jax.ShapeDtypeStruct(shape, kind)


MEGA = 2**20


def run(kernel, seqs, ins, in_specs, outs, out_specs, scratch=(), prefetch=(), room=56):
    return pl.pallas_call(
        kernel,
        grid_spec=pltpu.PrefetchScalarGridSpec(
            num_scalar_prefetch=len(prefetch),
            grid=(seqs,),
            in_specs=in_specs,
            out_specs=out_specs,
            scratch_shapes=list(scratch),
        ),
        out_shape=outs,
        compiler_params=pltpu.CompilerParams(vmem_limit_bytes=room * MEGA),
    )(*prefetch, *ins)


def unit_plan(seqs, heads):
    parts = lax.axis_size("tm")
    if parts <= heads:
        return heads // parts, seqs, 1
    return 1, seqs * heads // parts, parts // heads


def distance_hot(seq_total, bucket_count):
    limits = jnp.array(boundaries(seq_total), jnp.int32)
    places = jnp.arange(seq_total, dtype=jnp.int32)
    bucket = jnp.sum((places[:, None] >= limits[None, :]).astype(jnp.int32), axis=1)
    return (bucket[:, None] == jnp.arange(bucket_count, dtype=jnp.int32)[None, :]).astype(FLOAT)


def bias_strip(table, hot, nh, split, local_frames):
    seq_total = hot.shape[0]
    first = lax.axis_index("tm") // split * nh
    mine = lax.dynamic_slice_in_dim(table, first, nh, 1)
    per = jnp.dot(hot, mine, precision=HIGHEST).T
    shifted = [
        jnp.pad(per, ((0, 0), (local_frames + s, 0)), constant_values=NEGATIVE)[
            :, : local_frames + seq_total
        ]
        for s in range(8)
    ]
    return make_strip(jnp.stack(shifted, 1), local_frames, seq_total)


def table_grad(diagonals, hot, nh, split, heads):
    seq_total = hot.shape[0]
    per = sum(
        jnp.pad(diagonals[:, s, s:], ((0, 0), (0, s))) for s in range(8)
    )
    mine = jnp.dot(hot.T, per.T, precision=HIGHEST)
    first = lax.axis_index("tm") // split * nh
    return lax.dynamic_update_slice_in_dim(
        jnp.zeros((hot.shape[1], heads), FLOAT), mine, first, 1
    )


def swap(values):
    return lax.all_to_all(values, "tm", 0, 0, tiled=True)


def total_over(packed):
    sent = packed.reshape((-1,) + packed.shape[2:])
    part = lax.psum_scatter(sent, "rows", scatter_dimension=0, tiled=True)
    return lax.psum(part, "tm")


def body(
    frames, cotangent, lengths,
    early_gain, early_shift, early_up, early_down,
    attend_gain, attend_shift, attend_input, attend_output, distance_bias,
    convolve_gain, convolve_shift, convolve_input, depthwise, inner_gain, inner_shift, convolve_output,
    late_gain, late_shift, late_up, late_down, final_gain, final_shift,
):
    seqs, rows, width = frames.shape
    heads = distance_bias.shape[1]
    count = lax.axis_size("rows")
    parts = lax.axis_size("tm")
    hidden = early_up.shape[1]
    channels = convolve_output.shape[0]
    nh, recs, split = unit_plan(seqs, heads)
    units = heads // nh
    flat = lambda v: v.reshape(1, -1)

    def wide(kinds):
        return spot((units, split, kinds, recs, rows, 128), BF)

    ins = (
        frames, flat(early_gain), flat(early_shift), early_up, early_down,
        flat(attend_gain), flat(attend_shift), attend_input,
    )
    outs = (
        spot((seqs, rows, width)), spot((seqs, rows, width), BF), spot((seqs, rows, hidden), BF),
        spot((seqs, rows, hidden), BF), spot((seqs, rows, width), BF), wide(3),
    )
    x1, h1, a1, sp1, h2, qkv = run(
        functools.partial(open_kernel, nh=nh), seqs, ins,
        [per_rec(frames)] + [whole(v) for v in ins[1:]],
        outs, [per_rec(v) for v in outs[:5]] + [per_unit(outs[5], recs)],
    )
    units_in = swap(qkv.reshape(parts, 3, recs, rows, 128))
    mine = lax.dynamic_slice_in_dim(lengths, lax.axis_index("tm") % split * recs, recs, 0)
    hot = distance_hot(rows * parts, distance_bias.shape[0])
    strip = bias_strip(distance_bias.astype(FLOAT), hot, nh, split, rows)
    out, out_t, lse = attn_fwd(mine, units_in, strip, nh)
    back = swap(out).reshape(units, split, recs, rows, 128)

    first = lax.axis_index("tm") * rows
    limits = jnp.concatenate([lengths, first[None].astype(jnp.int32)])
    ins = (back, x1, attend_output, flat(convolve_gain), flat(convolve_shift), convolve_input)
    outs = (
        spot((seqs, rows, width), BF), spot((seqs, rows, width)), spot((seqs, rows, width), BF),
        spot((seqs, rows, channels), BF), spot((seqs, rows, channels), BF), spot((seqs, rows, channels), BF),
    )
    att, x2, h3, g, ga, gb = run(
        functools.partial(gate_kernel, nh=nh), seqs, ins,
        [per_unit(back, recs), per_rec(x1)] + [whole(v) for v in ins[2:]],
        outs, [per_rec(v) for v in outs], prefetch=(limits,),
    )
    halo = passed_along(g[:, rows - 16 :, :], "tm", 1)

    dep = jnp.pad(depthwise.astype(FLOAT).T, ((0, 1), (0, 0)))
    ins = (
        g, halo, x2, cotangent, dep, flat(inner_gain), flat(inner_shift), convolve_output,
        flat(late_gain), flat(late_shift), late_up, late_down, flat(final_gain), flat(final_shift),
    )
    height = (width * hidden * 2 + channels * width) // 512 // count
    outs = (
        spot((seqs, rows, width), BF), spot((seqs, rows, width)), spot((seqs, rows, channels), BF),
        spot((seqs, 16, channels), BF), spot((16, 512)), spot((16, channels)), spot((count, height, 512), BF),
    )
    tokens = seqs * rows
    layer_out, dx3, dg, dhalo, small_mid, ddep, pack_mid = run(
        middle_kernel, seqs, ins,
        [per_rec(v) for v in ins[:4]] + [whole(v) for v in ins[4:]],
        outs, [per_rec(v) for v in outs[:4]] + [whole(v) for v in outs[4:]],
        scratch=(
            pltpu.VMEM((rows + 16, channels), F32), pltpu.VMEM((rows, channels), F32),
            pltpu.VMEM((rows + 32, channels), F32), pltpu.VMEM((rows, channels), BF),
            pltpu.VMEM((tokens, width), BF), pltpu.VMEM((tokens, hidden), BF), pltpu.VMEM((rows, hidden), BF),
            pltpu.VMEM((tokens, hidden), BF), pltpu.VMEM((tokens, width), BF),
            pltpu.VMEM((tokens, channels), BF), pltpu.VMEM((tokens, width), BF),
        ),
    )
    returned = passed_along(dhalo, "tm", -1)

    ins = (dg, returned, ga, gb, dx3, x2, flat(convolve_gain), convolve_input, attend_output)
    outs = (
        spot((seqs, rows, width)), spot((seqs, rows, 2 * channels), BF), spot((seqs, rows, width), BF),
        spot((units, split, recs, rows, 128), BF), spot((8, 512)),
    )
    dx2, du, dy2, do, small_gate = run(
        functools.partial(ungate_kernel, nh=nh), seqs, ins,
        [per_rec(v) for v in ins[:6]] + [whole(v) for v in ins[6:]],
        outs, [per_rec(v) for v in outs[:3]] + [per_unit(outs[3], recs), whole(outs[4])],
        scratch=(pltpu.VMEM((rows, channels), F32),),
    )
    grad_units = swap(do.reshape(parts, recs, rows, 128))
    merge = lambda v: v.reshape(tokens, -1)
    ins = (merge(h3), merge(du), merge(att), merge(dy2))
    outs = spot((count, (2 * channels * width + width * width) // 512 // count, 512), BF)
    pack_gate = run(weights_kernel, 1, ins, [whole(v) for v in ins], outs, whole(outs))
    grad_own, diagonals = attn_bwd(mine, units_in, grad_units, out_t, lse, strip, nh)
    grad_back = swap(grad_own).reshape(units, split, 3, recs, rows, 128)

    ins = (
        grad_back, h2, x1, dx2, frames, h1, a1, sp1,
        flat(early_gain), early_up, early_down, flat(attend_gain), attend_input,
    )
    height = (width * hidden * 2 + width * 3 * width) // 512 // count
    outs = (spot((seqs, rows, width), BF), spot((8, 512)), spot((count, height, 512), BF))
    dx0, small_open, pack_open = run(
        functools.partial(close_kernel, nh=nh), seqs, ins,
        [per_unit(grad_back, recs)] + [per_rec(v) for v in ins[1:8]] + [whole(v) for v in ins[8:]],
        outs, [per_rec(outs[0])] + [whole(v) for v in outs[1:]],
        scratch=(
            pltpu.VMEM((tokens, 3 * width), BF), pltpu.VMEM((tokens, width), BF), pltpu.VMEM((tokens, width), BF),
            pltpu.VMEM((tokens, hidden), BF), pltpu.VMEM((tokens, hidden), BF), pltpu.VMEM((tokens, width), BF),
        ),
    )
    grad_table = table_grad(diagonals, hot, nh, split, heads)

    lines = jnp.concatenate([small_open[:4], small_gate[:2], small_mid[:10]], axis=0)
    lines = jnp.transpose(lines.reshape(8, 2, count, 256 // count * 2 // 2), (2, 0, 1, 3)) if False else lines
    totals_mid = total_over(pack_mid)
    totals_gate = total_over(pack_gate)
    shape_small = (small_open, small_gate, small_mid, ddep, grad_table)
    small = pack_small(*shape_small, count)
    extra = small.shape[1]
    totals_open = total_over(jnp.concatenate([pack_open, small], axis=1))
    return finish(
        layer_out, dx0, totals_mid.astype(FLOAT), totals_gate.astype(FLOAT), totals_open.astype(FLOAT),
        count, width, hidden, channels, depthwise.shape[1], distance_bias.shape,
    )


def vectors(small_open, small_gate, small_mid):
    return [
        small_open[0:1], small_open[1:2], small_open[2:3], small_open[3:4],
        small_gate[0:1], small_gate[1:2], small_mid[2:4], small_mid[4:6],
        small_mid[6:7], small_mid[7:8], small_mid[8:9], small_mid[9:10],
    ]


def pack_small(small_open, small_gate, small_mid, ddep, grad_table, count):
    shares = [v.reshape(count, -1) for v in vectors(small_open, small_gate, small_mid)]
    shares.append(jnp.transpose(ddep.reshape(16, count, -1), (1, 0, 2)).reshape(count, -1))
    shares.append(grad_table.reshape(count, -1))
    line = jnp.concatenate(shares, axis=1)
    line = jnp.pad(line, ((0, 0), (0, -line.shape[1] % (64 * 512))))
    return line.reshape(count, -1, 512).astype(BF)


def columns(block, blocks):
    return jnp.concatenate(jnp.split(block, blocks, axis=0), axis=1)


def finish(layer_out, dx0, mid, gate, opened, count, width, hidden, channels, taps, table_shape):
    share = width // count
    wide = hidden // 512
    late_up = columns(mid[: share * wide], wide)
    late_down = mid[share * wide : share * wide + hidden // count]
    conv_out = mid[share * wide + hidden // count :]
    conv_in = columns(gate[: share * (2 * channels // 512)], 2 * channels // 512)
    attend_out = gate[share * (2 * channels // 512) :]
    attend_in = columns(opened[: 3 * share], 3)
    at = 3 * share
    early_up = columns(opened[at : at + share * wide], wide)
    at += share * wide
    early_down = opened[at : at + hidden // count]
    at += hidden // count
    line = opened[at:].reshape(-1)
    sizes = [share] * 6 + [channels // count] * 2 + [share] * 4
    got = []
    at = 0
    for size in sizes:
        got.append(line[at : at + size])
        at += size
    depth = line[at : at + 16 * channels // count].reshape(16, -1)[:taps].T
    at += 16 * channels // count
    table = line[at : at + table_shape[0] * table_shape[1] // count].reshape(-1, table_shape[1])
    return (
        layer_out, dx0, got[0], got[1], early_up, early_down, got[2], got[3], attend_in, attend_out, table,
        got[4], got[5], conv_in, depth, got[6], got[7], conv_out,
        got[8], got[9], late_up, late_down, got[10], got[11],
    )


def solution(mesh):
    placed = (
        P("rows", "tm", None),
        P("rows", "tm", None),
        P("rows"),
        P(),
        P(),
        P(),
        P(),
        P(),
        P(),
        P(),
        P(),
        P(),
        P(),
        P(),
        P(),
        P(),
        P(),
        P(),
        P(),
        P(),
        P(),
        P(),
        P(),
        P(),
        P(),
    )
    return jax.shard_map(
        body,
        mesh=mesh,
        in_specs=placed,
        out_specs=(
            P("rows", "tm", None),
            P("rows", "tm", None),
            P("rows"),
            P("rows"),
            P("rows", None),
            P("rows", None),
            P("rows"),
            P("rows"),
            P("rows", None),
            P("rows", None),
            P("rows", None),
            P("rows"),
            P("rows"),
            P("rows", None),
            P("rows", None),
            P("rows"),
            P("rows"),
            P("rows", None),
            P("rows"),
            P("rows"),
            P("rows", None),
            P("rows", None),
            P("rows"),
            P("rows"),
        ),
        check_vma=False,
    )
```

time: 1740 us -> 458 us (0.26)
  starting transfers between devices: 562 us -> 20.3 us
  waiting for transfers between devices: 568 us -> 217 us
  local copies, waits for them, and re-layouts: 247 us -> 33.3 us
  other arithmetic: 182 us -> 11.3 us
  Pallas kernels: 0 us -> 156 us
  matrix products: 106 us -> 1.22 us
  blocking collectives: 43.2 us -> 0 us
    ppermute x8 -> x0, starting transfers between devices: 316 us -> none  [from_behind(): return lax.ppermute(value, axis, pairs)]
    ppermute x10 -> x2, starting transfers between devices: 245 us -> 3.79 us  [passed_along(): return lax.ppermute(block, axis, route)]
    pallas_call x0 -> x9, Pallas kernels: none -> 156 us  [the longest x6 115 us: run(): pl.pallas_call(kernel, grid_spec=pltpu.PrefetchScalarGridSpec(num_scalar_...]
    ppermute x10 -> x2, waiting for transfers between devices: 161 us -> 7.29 us  [passed_along(): return lax.ppermute(block, axis, route)]
    reduce_scatter x8 -> x3, waiting for transfers between devices: 199 us -> 76.2 us  [total_over(): part = lax.psum_scatter(sent, 'rows', scatter_dimension=0, tiled=True)]
    dot_general x34 -> x2, matrix products: 106 us -> 1.22 us  [the longest x1 0.83 us: table_grad(): mine = jnp.dot(hot.T, per.T, precision=HIGHEST)]
    ppermute x8 -> x0, waiting for transfers between devices: 89.5 us -> none  [from_behind(): return lax.ppermute(value, axis, pairs)]
    all_gather x2 -> x0, waiting for transfers between devices: 81 us -> none  [the longest x1 41.2 us: attend_forward(): lax.all_gather(key_rows, 'tm', axis=1, tiled=True)]
  transfers between devices with their start and end apart: 30 -> 10, of which waited for: 26 -> 9; matrix products, arithmetic and copies ran while one was open for 16% -> 4% of each run, Pallas kernels for 0% -> 9%
where the time goes in v1:
time: 458 us; the launch traced here: 453 us
  waiting for transfers between devices  217 us (47%)
  Pallas kernels  156 us (34%)
  local copies, waits for them, and re-layouts  33.3 us (7%)
  starting transfers between devices  20.3 us (4%)
  between operations  14.5 us (3%)
  other arithmetic  11.3 us (2%)
    pallas_call x6, Pallas kernels, run(): pl.pallas_call(kernel, grid_spec=pltpu.PrefetchScalarGridSpec(num_scalar_...  115 us
    reduce_scatter x3, waiting for transfers between devices, total_over(): part = lax.psum_scatter(sent, 'rows', scatter_dimension=0, tiled=True)  76.2 us
    all_to_all x4, waiting for transfers between devices, swap(): return lax.all_to_all(values, 'tm', 0, 0, tiled=True)  66.5 us
    psum x1, waiting for transfers between devices, total_over(): return lax.psum(part, 'tm')  66.2 us
    pallas_call x1, Pallas kernels, attn_bwd(): pl.pallas_call(functools.partial(bwd_kernel, nh=nh), grid_spec=gs, out_sh...  21.9 us
    pallas_call x1, Pallas kernels, attn_fwd(): pl.pallas_call(functools.partial(fwd_kernel, nh=nh, BQ=T), grid_spec=gs,...  17.9 us
    all_to_all x4, starting transfers between devices, swap(): return lax.all_to_all(values, 'tm', 0, 0, tiled=True)  16.4 us
    reshape x12, local copies, waits for them, and re-layouts, body(): flat = lambda v: v.reshape(1, -1)  9.62 us
  transfers between devices with their start and end apart: 10, of which 9 were waited for; matrix products, arithmetic and copies ran while one was open for 4% of the time, Pallas kernels for 9%

profile of v1, /device:TPU:0, one launch (start us, length us, event | category | flops | bytes accessed | tf_op | source)
XLA Modules:
  0.0 453.1 jit_solution(11609273264324365441)
XLA Ops:
  7.2 1.3 reshape.195.g1
  8.5 1.3 reshape.197.g2
  9.7 1.3 reshape.196.s1
  11.0 1.3 reshape.198.s2
  12.3 11.0 %shard_map.433 = (f32[2,384,512]{2,1,0:T(8,128)}, bf16[2,384,512]{2,1,0:T(8,128)(2,1)}, bf16[2,384,2048]{2,1,0:T(8,128)(2,1)}, bf16[2,384,2048]{2,1,0:T(8,128)(2...) custom-call(bf16[2,384,512]{2,1,0:T(8,128)(2,1)} %x_ref.3, bf16[1,512]{1,0:T(2,128)(2,1)} %reshape.195.g1, ...), custom_call_target="tpu_custom_call" | custom-call | tf_op jit(solution)/shard_map/pallas_call | solution.py:543
  23.3 5.2 %all-to-all-start = ((bf16[4,3,2,384,128]{4,3,2,1,0:T(8,128)(2,1)}), bf16[4,3,2,384,128]{4,3,2,1,0:T(8,128)(2,1)S(1)}, u32[]{:S(2)}, u32[]{:S(2)}) async-start(bf16[4,3,2,384,128]{4,3,2,1,0:T(8,128)(2,1)} %bitcast.67), calls=%async_computation | async-start | bytes 4718592 | tf_op jit(solution)/shard_map/all_to_all | solution.py:598
  29.5 0.5 shard_map.434.b_ref
  30.1 2.1 copy-done.2
  32.2 23.9 %all-to-all-done.x_ref = bf16[4,3,2,384,128]{4,3,2,1,0:T(8,128)(2,1)S(1)} async-done(((bf16[4,3,2,384,128]{4,3,2,1,0:T(8,128)(2,1)}), bf16[4,3,2,384,128]{4,3,2,1,0:T(8,128)(2,1)S(1)}, u32[]{:S(2)}, u32[]{:S(2)}) %all-to-all-start) | async-done | bytes 2359328 | tf_op jit(solution)/shard_map/all_to_all | solution.py:598
  56.2 1.4 copy-done.3
  57.6 17.9 %shard_map.435 = (bf16[4,2,384,128]{3,2,1,0:T(8,128)(2,1)}, f32[2,4,128,384]{3,2,1,0:T(8,128)}, f32[2,2,4,1,384]{4,3,2,1,0:T(1,128)}) custom-call(s32[2]{0:T(128)} %len_ref.1, bf16[4,3,2,384,128]{4,3,2,1,0:T(8,128)(2,1)} %copy-done.3, f32[2,384,1536]{2,1,0:T(8,128)} %copy-done.2), custom_call_target="tpu_custom_call" | custom-call | tf_op jit(solution)/shard_map/pallas_call | solution.py:102
  75.4 3.5 all-to-all-start.1
  79.0 0.6 reshape.201.g3
  79.6 0.6 reshape.202.s3
  80.2 0.5 reshape.205.lg
  80.7 0.6 reshape.206.ls
  81.3 0.5 reshape.207.fg
  81.9 0.5 reshape.208.fs
  82.4 0.6 reshape.203.ig
  83.0 0.6 reshape.204.si
  83.6 0.6 pad_add_fusion.len_ref
  84.2 5.8 %all-to-all-done.1 = bf16[4,2,384,128]{3,2,1,0:T(8,128)(2,1)S(1)} async-done(((bf16[4,2,384,128]{3,2,1,0:T(8,128)(2,1)}), bf16[4,2,384,128]{3,2,1,0:T(8,128)(2,1)S(1)}, u32[]{:S(2)}, u32[]{:S(2)}) %all-to-all-start.1) | async-done | bytes 786464 | tf_op jit(solution)/shard_map/all_to_all | solution.py:598
  90.0 0.9 copy-done.6
  90.9 8.1 %shard_map.436 = (bf16[2,384,512]{2,1,0:T(8,128)(2,1)}, f32[2,384,512]{2,1,0:T(8,128)}, bf16[2,384,512]{2,1,0:T(8,128)(2,1)}, bf16[2,384,1024]{2,1,0:T(8,128)(2,...) custom-call(s32[3]{0:T(128)} %pad_add_fusion.len_ref, bf16[4,1,2,384,128]{4,3,2,1,0:T(8,128)(2,1)} %bitcast.66, ...), custom_call_target="tpu_custom_call" | custom-call | tf_op jit(solution)/shard_map/pallas_call | solution.py:543
  99.0 0.8 slice.189
  99.9 2.5 collective-permute-start
  102.4 0.6 pad_convert_fusion.dep
  103.0 1.2 collective-permute-done.halo_ref
  104.3 0.6 copy-done.15
  104.9 63.1 %shard_map.437 = (bf16[2,384,512]{2,1,0:T(8,128)(2,1)}, f32[2,384,512]{2,1,0:T(8,128)}, bf16[2,384,1024]{2,1,0:T(8,128)(2,1)}, bf16[2,16,1024]{2,1,0:T(8,128)(2,...) custom-call(bf16[2,384,1024]{2,1,0:T(8,128)(2,1)} %get-tuple-element.59.g_ref, ...), custom_call_target="tpu_custom_call" | custom-call | tf_op jit(solution)/shard_map/pallas_call | solution.py:543
  168.0 1.3 collective-permute-start.1
  169.3 6.1 %collective-permute-done.1.back_ref = bf16[2,16,1024]{2,1,0:T(8,128)(2,1)S(1)} collective-permute-done((bf16[2,16,1024]{2,1,0:T(8,128)(2,1)}, bf16[2,16,1024]{2,1,0:T(8,128)(2,1)S(1)}, u32[]{:S(2)}, u32[]{:S(2)}) %collective-permute-start.1) | collective-permute-done | bytes 65568 | tf_op jit(solution)/shard_map/ppermute | solution.py:23
  175.3 0.6 copy-done.16
  176.0 7.8 %shard_map.438 = (f32[2,384,512]{2,1,0:T(8,128)}, bf16[2,384,2048]{2,1,0:T(8,128)(2,1)}, bf16[2,384,512]{2,1,0:T(8,128)(2,1)}, bf16[4,1,2,384,128]{4,3,2,1,0:T(8,128)(2,1)}, f32[8,512]{1,0:T(8,128)}) custom-call(bf16[2,384,1024]{2,1,0:T(8,128)(2,1)} %get-tuple-element.62.dg_ref, bf16[2,16,1024]{2,1,0:T(8,128)(2,1)} %copy-done.16, ...), custom_call_target="tpu_custom_call" | custom-call | tf_op jit(solution)/shard_map/pallas_call | solution.py:543
  183.8 6.3 %shard_map.441 = bf16[8,320,512]{2,1,0:T(8,128)(2,1)} custom-call(bf16[768,512]{1,0:T(8,128)(2,1)} %bitcast.71, bf16[768,2048]{1,0:T(8,128)(2,1)} %bitcast.65, bf16[768,512]{1,0:T(8,128)(2,1)} %bitcast.70, bf16[768,512]{1,0:T(8,128)(2,1)} %bitcast.72), custom_call_target="tpu_custom_call" | custom-call | tf_op jit(solution)/shard_map/pallas_call | solution.py:543
  190.2 0.7 reduce-scatter.8.cloned.1.call-update
  190.9 3.9 all-to-all-start.2
  195.5 10.8 %all-to-all-done.2.do_ref = bf16[4,2,384,128]{3,2,1,0:T(8,128)(2,1)S(1)} async-done(((bf16[4,2,384,128]{3,2,1,0:T(8,128)(2,1)}), bf16[4,2,384,128]{3,2,1,0:T(8,128)(2,1)S(1)}, u32[]{:S(2)}, u32[]{:S(2)}) %all-to-all-start.2) | async-done | bytes 786464 | tf_op jit(solution)/shard_map/all_to_all | solution.py:598
  206.3 0.9 copy-done.7
  207.2 21.9 %shard_map.439 = (bf16[4,3,2,384,128]{4,3,2,1,0:T(8,128)(2,1)}, f32[2,8,1536]{2,1,0:T(8,128)}) custom-call(s32[2]{0:T(128)} %len_ref.1, bf16[4,3,2,384,128]{4,3,2,1,0:T(8,128)(2,1)} %copy-done.3, bf16[4,2,384,128]{3,2,1,0:T(8,128)(2,1)} %copy-done.7, f32[2,4,128,384]{3,2,1,0:T(8,128)} %get-tuple-element.68.ot_ref, ...), custom_call_target="tpu_custom_call" | custom-call | tf_op jit(solution)/shard_map/pallas_call | solution.py:184
  229.1 3.8 all-to-all-start.3
  233.6 0.8 fusion.2
  234.9 25.9 %all-to-all-done.3 = bf16[4,3,2,384,128]{4,3,2,1,0:T(8,128)(2,1)S(1)} async-done(((bf16[4,3,2,384,128]{4,3,2,1,0:T(8,128)(2,1)}), bf16[4,3,2,384,128]{4,3,2,1,0:T(8,128)(2,1)S(1)}, u32[]{:S(2)}, u32[]{:S(2)}) %all-to-all-start.3) | async-done | bytes 2359328 | tf_op jit(solution)/shard_map/all_to_all | solution.py:598
  260.8 1.4 copy-done.4
  262.2 19.0 %shard_map.440 = (bf16[2,384,512]{2,1,0:T(8,128)(2,1)}, f32[8,512]{1,0:T(8,128)}, bf16[8,704,512]{2,1,0:T(8,128)(2,1)}) custom-call(bf16[4,1,3,2,384,128]{5,4,3,2,1,0:T(8,128)(2,1)} %bitcast.63, bf16[2,384,512]{2,1,0:T(8,128)(2,1)} %get-tuple-element.71.h2_ref, f32[2,384,512]{2,1,0:T(8,128)} %get-tuple-element.58.x1_ref, ...), custom_call_target="tpu_custom_call" | custom-call | tf_op jit(solution)/shard_map/pallas_call | solution.py:543
  281.3 0.7 convert.57
  282.7 5.7 %pad_maximum_fusion = bf16[8,768,512]{2,1,0:T(8,128)(2,1)} fusion(bf16[8,64,512]{2,1,0:T(8,128)(2,1)S(1)} %bitcast.68, bf16[8,704,512]{2,1,0:T(8,128)(2,1)} %get-tuple-element.77), kind=kLoop, calls=%fused_computation | loop fusion | flops 12582912 | bytes 12582912 | tf_op jit(solution)/shard_map/concatenate | solution.py:729
  288.5 5.6 %reduce-scatter.8.cloned.1.call-done = bf16[640,512]{1,0:T(8,128)(2,1)} async-done(((bf16[5120,512]{1,0:T(8,128)(2,1)}), bf16[640,512]{1,0:T(8,128)(2,1)}) %reduce-scatter.8.cloned.1.call-update) | async-done | bytes 655376 | tf_op jit(solution)/shard_map/reduce_scatter | solution.py:603
  294.1 70.5 %reduce-scatter.4.cloned.1.call-done = bf16[768,512]{1,0:T(8,128)(2,1)} async-done(((bf16[6144,512]{1,0:T(8,128)(2,1)}), bf16[768,512]{1,0:T(8,128)(2,1)}) %reduce-scatter.4.cloned.1.call-update) | async-done | bytes 786448 | tf_op jit(solution)/shard_map/reduce_scatter | solution.py:603
  364.7 66.2 %all-reduce.20.cloned.1.call-done = (bf16[768,512]{1,0:T(8,128)(2,1)}, bf16[320,512]{1,0:T(8,128)(2,1)}, bf16[640,512]{1,0:T(8,128)(2,1)}) async-done(((bf16[768,512]{1,0:T(8,128)(2,1)}, bf16[320,512]{1,0:T(8,128)(2,1)}, bf16[640,512]{1,0:T(8,128)(2,1)}), (bf16[768,512]{1,0:T(8,128)(2,1)}, bf16[320,512]{1,0:T(8,128)(2,1)}, bf16[640,512]{1,0:T(8,128)(2,1)})) %all-reduce.20.cloned.1.call-update) | async-done | bytes 1769488 | tf_op jit(solution)/shard_map/psum | solution.py:604
  430.9 1.7 slice.263
  432.6 1.8 slice.266
  434.4 1.8 slice.253
  436.3 0.9 fusion.23
  438.0 0.6 fusion.26
  438.6 0.7 slice.221
  439.3 1.1 slice.217
  440.5 0.7 fusion.25
  441.2 1.3 slice_bitcast_fusion.7
  442.5 0.6 slice.257
  443.1 0.8 pad_maximum_fusion.4
  443.9 0.8 pad_maximum_fusion.2
  444.7 0.8 pad_maximum_fusion.1
  445.5 0.8 pad_maximum_fusion.3
  (114 shorter events, 4.5 us)
Async XLA Ops:
  7.2 21.4 %copy-start = (bf16[32,8]{0,1:T(8,128)(2,1)S(1)}, bf16[32,8]{0,1:T(8,128)(2,1)}, u32[]{:S(2)}) copy-start(bf16[32,8]{0,1:T(8,128)(2,1)} %param.37) | copy-start | bytes 1540
  23.3 5.2 %copy-start.30 = (s32[31]{0:T(128)S(1)}, s32[31]{0:T(128)}, u32[]{:S(2)}) copy-start(s32[31]{0:T(128)} %constant.41.clone) | copy-start | bytes 376
  23.3 32.9 %all-to-all-start = ((bf16[4,3,2,384,128]{4,3,2,1,0:T(8,128)(2,1)}), bf16[4,3,2,384,128]{4,3,2,1,0:T(8,128)(2,1)S(1)}, u32[]{:S(2)}, u32[]{:S(2)}) async-start(bf16[4,3,2,384,128]{4,3,2,1,0:T(8,128)(2,1)} %bitcast.67), calls=%async_computation | async-start | bytes 4718592 | tf_op jit(solution)/shard_map/all_to_all | solution.py:598
  30.0 2.1 copy-start.2
  32.2 46.8 %copy-start.24 = (bf16[512]{0:T(512)(128)(2,1)S(1)}, bf16[512]{0:T(512)(128)(2,1)}, u32[]{:S(2)}) copy-start(bf16[512]{0:T(512)(128)(2,1)} %param.38) | copy-start | bytes 3076
  32.2 47.4 %copy-start.25 = (bf16[512]{0:T(512)(128)(2,1)S(1)}, bf16[512]{0:T(512)(128)(2,1)}, u32[]{:S(2)}) copy-start(bf16[512]{0:T(512)(128)(2,1)} %param.39) | copy-start | bytes 3076
  32.2 48.0 %copy-start.26 = (bf16[512]{0:T(512)(128)(2,1)S(1)}, bf16[512]{0:T(512)(128)(2,1)}, u32[]{:S(2)}) copy-start(bf16[512]{0:T(512)(128)(2,1)} %param.45) | copy-start | bytes 3076
  32.2 48.5 %copy-start.27 = (bf16[512]{0:T(512)(128)(2,1)S(1)}, bf16[512]{0:T(512)(128)(2,1)}, u32[]{:S(2)}) copy-start(bf16[512]{0:T(512)(128)(2,1)} %param.46) | copy-start | bytes 3076
  32.2 49.1 %copy-start.28 = (bf16[512]{0:T(512)(128)(2,1)S(1)}, bf16[512]{0:T(512)(128)(2,1)}, u32[]{:S(2)}) copy-start(bf16[512]{0:T(512)(128)(2,1)} %param.49) | copy-start | bytes 3076
  32.2 49.7 %copy-start.29 = (bf16[512]{0:T(512)(128)(2,1)S(1)}, bf16[512]{0:T(512)(128)(2,1)}, u32[]{:S(2)}) copy-start(bf16[512]{0:T(512)(128)(2,1)} %param.50) | copy-start | bytes 3076
  32.2 50.2 %copy-start.22 = (bf16[1024]{0:T(1024)(128)(2,1)S(1)}, bf16[1024]{0:T(1024)(128)(2,1)}, u32[]{:S(2)}) copy-start(bf16[1024]{0:T(1024)(128)(2,1)} %param.42) | copy-start | bytes 6148
  32.2 50.8 %copy-start.23 = (bf16[1024]{0:T(1024)(128)(2,1)S(1)}, bf16[1024]{0:T(1024)(128)(2,1)}, u32[]{:S(2)}) copy-start(bf16[1024]{0:T(1024)(128)(2,1)} %param.43) | copy-start | bytes 6148
  32.2 51.4 %copy-start.21 = (s32[2]{0:T(128)S(1)}, s32[2]{0:T(128)}, u32[]{:S(2)}) copy-start(s32[2]{0:T(128)} %len_ref.1) | copy-start | bytes 28
  56.2 1.4 copy-start.3
  75.4 14.6 %all-to-all-start.1 = ((bf16[4,2,384,128]{3,2,1,0:T(8,128)(2,1)}), bf16[4,2,384,128]{3,2,1,0:T(8,128)(2,1)S(1)}, u32[]{:S(2)}, u32[]{:S(2)}) async-start(bf16[4,2,384,128]{3,2,1,0:T(8,128)(2,1)} %get-tuple-element.57), calls=%async_computation.1 | async-start | bytes 1572864 | tf_op jit(solution)/shard_map/all_to_all | solution.py:598
  78.9 209.6 %reduce-scatter.6.cloned.1.call-start = ((), (), s32[]{:S(2)}) async-start(), calls=%async_computation.8 | async-start | bytes 2949120 | tf_op jit(solution)/shard_map/reduce_scatter | solution.py:603
  90.0 0.9 copy-start.6
  90.9 11.4 %copy-start.18 = (bf16[1024,15]{0,1:T(8,128)(2,1)S(1)}, bf16[1024,15]{0,1:T(8,128)(2,1)}, u32[]{:S(2)}) copy-start(bf16[1024,15]{0,1:T(8,128)(2,1)} %param.41) | copy-start | bytes 92164
  99.9 4.4 collective-permute-start
  104.3 0.6 copy-start.15
  168.0 7.4 %collective-permute-start.1 = (bf16[2,16,1024]{2,1,0:T(8,128)(2,1)}, bf16[2,16,1024]{2,1,0:T(8,128)(2,1)S(1)}, u32[]{:S(2)}, u32[]{:S(2)}) collective-permute-start(bf16[2,16,1024]{2,1,0:T(8,128)(2,1)} %get-tuple-element.63), channel_id=1, source_target_pairs={{1,0},{2,1},{3,2},{5,4},{6,5},{7,6},{9,8},{10,9},{11,10},{13,12},{... | collective-permute-start | bytes 196616 | tf_op jit(solution)/shard_map/ppermute | solution.py:23
  175.3 0.6 copy-start.16
  190.1 104.0 %reduce-scatter.8.cloned.1.call-start = ((), (), s32[]{:S(2)}) async-start(), calls=%async_computation.9 | async-start | bytes 5898240 | tf_op jit(solution)/shard_map/reduce_scatter | solution.py:603
  190.1 0.8 copy-start.19
  190.1 5.1 %copy-start.17 = (f32[16,1024]{1,0:T(8,128)S(1)}, f32[16,1024]{1,0:T(8,128)}, u32[]{:S(2)}) copy-start(f32[16,1024]{1,0:T(8,128)} %get-tuple-element.81) | copy-start | bytes 196612
  190.2 5.1 %copy-start.20 = (f32[8,512]{1,0:T(8,128)S(1)}, f32[8,512]{1,0:T(8,128)}, u32[]{:S(2)}) copy-start(f32[8,512]{1,0:T(8,128)} %get-tuple-element.79) | copy-start | bytes 49156
  190.9 15.4 %all-to-all-start.2 = ((bf16[4,2,384,128]{3,2,1,0:T(8,128)(2,1)}), bf16[4,2,384,128]{3,2,1,0:T(8,128)(2,1)S(1)}, u32[]{:S(2)}, u32[]{:S(2)}) async-start(bf16[4,2,384,128]{3,2,1,0:T(8,128)(2,1)} %bitcast.4), calls=%async_computation.2 | async-start | bytes 1572864 | tf_op jit(solution)/shard_map/all_to_all | solution.py:598
  206.3 0.9 copy-start.7
  229.1 3.8 copy-start.14
  229.1 31.7 %all-to-all-start.3 = ((bf16[4,3,2,384,128]{4,3,2,1,0:T(8,128)(2,1)}), bf16[4,3,2,384,128]{4,3,2,1,0:T(8,128)(2,1)S(1)}, u32[]{:S(2)}, u32[]{:S(2)}) async-start(bf16[4,3,2,384,128]{4,3,2,1,0:T(8,128)(2,1)} %get-tuple-element.70), calls=%async_computation.3 | async-start | bytes 4718592 | tf_op jit(solution)/shard_map/all_to_all | solution.py:598
  232.9 131.8 %reduce-scatter.4.cloned.1.call-start = ((), (), s32[]{:S(2)}) async-start(), calls=%async_computation.7 | async-start | bytes 7077888 | tf_op jit(solution)/shard_map/reduce_scatter | solution.py:603
  260.8 1.4 copy-start.4
  288.4 142.5 %all-reduce.20.cloned.1.call-start = ((), (), s32[]{:S(2)}) async-start(), calls=%async_computation.10 | async-start | bytes 3538944 | tf_op jit(solution)/shard_map/psum | solution.py:604
  430.9 5.4 %copy-start.5 = (bf16[768,512]{1,0:T(8,128)(2,1)S(1)}, bf16[768,512]{1,0:T(8,128)(2,1)}, u32[]{:S(2)}) copy-start(bf16[768,512]{1,0:T(8,128)(2,1)} %get-tuple-element.98) | copy-start | bytes 2359300
  430.9 5.4 %copy-start.8 = (bf16[640,512]{1,0:T(8,128)(2,1)S(1)}, bf16[640,512]{1,0:T(8,128)(2,1)}, u32[]{:S(2)}) copy-start(bf16[640,512]{1,0:T(8,128)(2,1)} %get-tuple-element.100) | copy-start | bytes 1966084
  437.2 3.3 copy-start.9
  440.4 4.3 copy-start.10
  440.4 4.3 copy-start.11
  440.4 4.3 copy-start.12
  440.4 4.3 copy-start.13
  440.5 5.9 %copy-start.1 = (bf16[32,8]{0,1:T(8,128)(2,1)S(1)}, bf16[32,8]{0,1:T(8,128)(2,1)}, u32[]{:S(2)}) copy-start(bf16[32,8]{0,1:T(8,128)(2,1)} %param.37) | copy-start | bytes 1540
Sparse Core Ops, SparseCore 0:
  190.2 42.5 reduce-scatter.5
  235.1 58.9 reduce-scatter.7
  296.4 68.1 reduce-scatter.3
  367.9 62.9 all-reduce.19
